TPU v7x, 256 devices: a whole 4x4x8 slice. The times are simulated.
256 devices in a mesh: ctx: 64 (over y, z, core), heads: 4 (over x).
Axes of the slice: x: 4, y: 4, z: 8, core: 2. Of those that a mesh axis runs over, the one named last changes fastest.
Arguments:
- q_in: bfloat16 [8192, 2048], P('ctx', 'heads'), may hold values from -6 to 6
- k_in: bfloat16 [8192, 2048], P('ctx', 'heads'), may hold values from -6 to 6
- v_in: bfloat16 [8192, 4096], P('ctx', 'heads'), may hold values from -6 to 6
- conv_q: bfloat16 [4, 2048], P(None, 'heads'), may hold values from -3 to 3
- conv_k: bfloat16 [4, 2048], P(None, 'heads'), may hold values from -3 to 3
- conv_v: bfloat16 [4, 4096], P(None, 'heads'), may hold values from -3 to 3
- a_in: float32 [8192, 32], P('ctx', 'heads')
- b_in: float32 [8192, 32], P('ctx', 'heads'), as said below
- a_log: float32 [32], P('heads')
- dt_bias: float32 [32], P('heads'), may hold values from -2 to 2
- norm_weight: float32 [128], replicated, may hold values from 0.1 to 1.9
- z_in: bfloat16 [8192, 4096], P('ctx', 'heads'), may hold values from -6 to 6
- out_weight: bfloat16 [4096, 2048], P('heads'), may hold values from -0.09375 to 0.09375
Outputs:
- mixed: float32 [8192, 2048], P('ctx', 'heads')
Inputs may be any that keep to these rules, and one draw needn't show every extreme that they name: `b_in`: write strength logits.
All inputs are finite; a program needn't handle non-finite values.
Results may differ from a plain program's by a relative error of at most 0.0039.
Values may be sent and summed in bfloat16 or wider, within the bound.
A program may use at most 192 MiB of HBM per device.

v0:
```python
import math

import jax
import jax.numpy as jnp
from jax import lax
from jax.sharding import PartitionSpec as P

DK = 128
DV = 128


highest = lax.Precision.HIGHEST


def shifted(value, axis, steps):
    count = lax.axis_size(axis)
    leading, last = (max(0, -steps), min(count, count - steps))
    return lax.ppermute(value, axis, [(source, source + steps) for source in range(leading, last)])


def carried_in(value, axis, join, neutral):
    count, mine = (lax.axis_size(axis), lax.axis_index(axis))
    pieces = jax.tree.map(lambda part: lax.all_gather(part, axis), value)
    running = jax.tree.map(
        lambda part, zero: jnp.full_like(part, 0) + jnp.asarray(zero, part.dtype), value, neutral
    )

    def lap(position, running):
        longer = join(running, jax.tree.map(lambda part: part[position], pieces))
        return jax.tree.map(lambda new, old: jnp.where(position < mine, new, old), longer, running)

    return lax.fori_loop(0, count - 1, lap, running)


def conv_silu(rim_rows, rows_in, weights):
    joined = jnp.concatenate([rim_rows, rows_in], axis=0).astype(jnp.float32)
    length = rows_in.shape[0]
    total = jnp.zeros(rows_in.shape, jnp.float32)
    for offset in range(weights.shape[0]):
        total = total + weights[offset].astype(jnp.float32) * joined[offset : offset + length]
    return jax.nn.silu(total).astype(jnp.bfloat16)


def unit_norm(blocked):
    entries = blocked.astype(jnp.float32)
    return entries * lax.rsqrt(jnp.sum(entries * entries, axis=-1, keepdims=True) + 1e-06)


def span_step(state, queries, key_rows, values, logdecay, beta_rows):
    length = queries.shape[1]
    positions = jnp.arange(length)
    strict = positions[:, None] > positions[None, :]
    upto = positions[:, None] >= positions[None, :]
    cumulative = jnp.cumsum(logdecay, axis=1)
    gaps = cumulative[:, :, None] - cumulative[:, None, :]
    within = jnp.exp(jnp.where(upto[None], gaps, -jnp.inf))
    key_gram = jnp.einsum("htd,hjd->htj", key_rows, key_rows, precision=highest)
    lower_part = jnp.where(strict[None], beta_rows[:, :, None] * key_gram * within, 0.0)
    identity_m = jnp.eye(length, dtype=queries.dtype)
    negated = -lower_part
    inverse = identity_m[None] + negated
    powers = negated
    for level in range(max(1, (length - 1).bit_length()) - 1):
        powers = jnp.einsum("hij,hjk->hik", powers, powers, precision=highest)
        inverse = inverse + jnp.einsum("hij,hjk->hik", inverse, powers, precision=highest)
    start_decay = jnp.exp(cumulative)
    seen = jnp.einsum("htd,hvd->htv", key_rows, state, precision=highest)
    right_side = beta_rows[:, :, None] * (values - start_decay[:, :, None] * seen)
    writes = jnp.einsum("htj,hjv->htv", inverse, right_side, precision=highest)
    query_gram = jnp.einsum("htd,hjd->htj", queries, key_rows, precision=highest) * within
    outputs = start_decay[:, :, None] * jnp.einsum(
        "htd,hvd->htv", queries, state, precision=highest
    )
    outputs = outputs + jnp.einsum("htj,hjv->htv", query_gram, writes, precision=highest)
    tail_decay = jnp.exp(cumulative[:, -1:] - cumulative)
    new_state = jnp.exp(cumulative[:, -1])[:, None, None] * state
    new_state = new_state + jnp.einsum(
        "hjv,hjd->hvd", writes * tail_decay[:, :, None], key_rows, precision=highest
    )
    return (outputs, new_state)


def scan_spans(
    state, query_blocks, key_blocks, value_blocks, decay_blocks, beta_blocks, group_size, extra
):

    def advance(carried, inputs):
        query_block, key_block, value_block, decay_block, beta_block = inputs
        scale_q = query_block.shape[-1] ** (-0.5)
        queries = jnp.repeat(unit_norm(query_block) * scale_q, group_size, axis=1).transpose(
            1, 0, 2
        )
        key_rows = jnp.repeat(unit_norm(key_block), group_size, axis=1).transpose(1, 0, 2)
        values = value_block.astype(jnp.float32).transpose(1, 0, 2)
        if extra:
            values = jnp.concatenate(
                [values, jnp.zeros(values.shape[:2] + (extra,), jnp.float32)], axis=2
            )
        outputs, new_state = span_step(
            carried, queries, key_rows, values, decay_block.T, beta_block.T
        )
        return (new_state, outputs)

    return lax.scan(
        advance, state, (query_blocks, key_blocks, value_blocks, decay_blocks, beta_blocks)
    )


def gate_norm(core_out, gate_rows, weight):
    scaled = (
        core_out * lax.rsqrt(jnp.mean(core_out * core_out, axis=-1, keepdims=True) + 1e-06) * weight
    )
    gated = scaled.reshape(gate_rows.shape) * jax.nn.silu(gate_rows.astype(jnp.float32))
    return gated.astype(jnp.bfloat16)


def shards(
    q_in,
    k_in,
    v_in,
    conv_q,
    conv_k,
    conv_v,
    a_in,
    b_in,
    a_log,
    dt_bias,
    norm_weight,
    z_in,
    out_weight,
):
    tap_count = conv_q.shape[0]
    row_count = q_in.shape[0]
    key_heads = q_in.shape[1] // DK
    value_heads = v_in.shape[1] // DV
    group_size = value_heads // key_heads
    query_width = q_in.shape[1]
    rim_start = row_count - tap_count + 1
    last_rows = jnp.concatenate([q_in[rim_start:], k_in[rim_start:], v_in[rim_start:]], axis=1)
    rim_rows = shifted(last_rows, "ctx", 1)
    query_conv = conv_silu(rim_rows[:, :query_width], q_in, conv_q)
    key_conv = conv_silu(rim_rows[:, query_width : 2 * query_width], k_in, conv_k)
    value_conv = conv_silu(rim_rows[:, 2 * query_width :], v_in, conv_v)
    logdecay = -jnp.exp(a_log)[None, :] * jax.nn.softplus(a_in + dt_bias[None, :])
    beta_rows = jax.nn.sigmoid(b_in)
    block_len = math.gcd(64, row_count)
    block_count = row_count // block_len
    blocked = (
        query_conv.reshape(block_count, block_len, key_heads, DK),
        key_conv.reshape(block_count, block_len, key_heads, DK),
        value_conv.reshape(block_count, block_len, value_heads, DV),
        logdecay.reshape(block_count, block_len, value_heads),
        beta_rows.reshape(block_count, block_len, value_heads),
    )
    identity_k = jnp.broadcast_to(jnp.eye(DK, dtype=jnp.float32), (value_heads, DK, DK))
    start_state = jnp.concatenate(
        [jnp.zeros((value_heads, DV, DK), jnp.float32), identity_k], axis=1
    )
    final_state, outputs = scan_spans(
        start_state, blocked[0], blocked[1], blocked[2], blocked[3], blocked[4], group_size, DK
    )
    local_state = final_state[:, :DV]
    transition = final_state[:, DV:]

    def compose(earlier, later):
        joined_map = jnp.einsum("hij,hjk->hik", earlier[0], later[0], precision=highest)
        joined_state = (
            jnp.einsum("hvj,hjk->hvk", earlier[1], later[0], precision=highest) + later[1]
        )
        return (joined_map, joined_state)

    prefix = carried_in(
        (transition, local_state), "ctx", compose, (identity_k, jnp.zeros_like(local_state))
    )
    incoming = prefix[1]
    second_state, core_blocks = scan_spans(
        incoming, blocked[0], blocked[1], blocked[2], blocked[3], blocked[4], group_size, 0
    )
    core_out = core_blocks.transpose(0, 2, 1, 3).reshape(row_count, value_heads, DV)
    normed = gate_norm(core_out, z_in, norm_weight)
    partial_terms = jnp.dot(normed, out_weight, preferred_element_type=jnp.float32)
    return lax.psum_scatter(partial_terms, "heads", scatter_dimension=1, tiled=True)


def solution(mesh):
    in_specs = (
        P("ctx", "heads"),
        P("ctx", "heads"),
        P("ctx", "heads"),
        P(None, "heads"),
        P(None, "heads"),
        P(None, "heads"),
        P("ctx", "heads"),
        P("ctx", "heads"),
        P("heads"),
        P("heads"),
        P(),
        P("ctx", "heads"),
        P("heads", None),
    )
    out_specs = P("ctx", "heads")
    return jax.shard_map(shards, mesh=mesh, in_specs=in_specs, out_specs=out_specs, check_vma=False)
```

profile of v0, /device:TPU:25, one launch (start us, length us, event | category | flops | bytes accessed | tf_op | source)
XLA Modules:
  0.0 597.1 jit_solution(14248702488095616726)
XLA Ops:
  8.7 4.1 collective-permute-start
  19.8 18.7 %while.36 = (s32[]{:T(128)}, f32[8,256,128]{2,1,0:T(8,128)S(1)}, f32[2,64,8]{1,2,0:T(8,128)S(1)}, f32[2,64,8]{1,2,0:T(8,128)S(1)}, bf16[2,64,4,128]{3,1,2,0:T(8,...) while((s32[]{:T(128)}, f32[8,256,128]{2,1,0:T(8,128)S(1)}, ...), condition=%wide.region_3.4_spmd, body=%wide.region_0.3_spmd.sunk | while | flops 807092224 | bytes 10699049 | solution.py:104
  27.0 2.1 convolution_add_fusion.30
  36.4 2.1 convolution_add_fusion.30
  40.9 141.2 %all-gather.5.cloned.1.call-done = f32[512,128,128]{2,1,0:T(8,128)} async-done(((f32[8,128,128]{2,1,0:T(8,128)}), f32[512,128,128]{2,1,0:T(8,128)}) %all-gather.5.cloned.1.call-update) | async-done | bytes 33554448 | tf_op jit(solution)/shard_map/all_gather | solution.py:23
  182.1 142.3 %all-gather.7.cloned.1.call-done = f32[512,128,128]{2,1,0:T(8,128)} async-done(((f32[8,128,128]{2,1,0:T(8,128)}), f32[512,128,128]{2,1,0:T(8,128)}) %all-gather.7.cloned.1.call-update) | async-done | bytes 33554448 | tf_op jit(solution)/shard_map/all_gather | solution.py:23
  324.4 216.7 %while.38 = (s32[]{:T(128)}, f32[8,128,128]{1,2,0:T(8,128)S(1)}, s32[]{:T(128)}, f32[64,8,128,128]{3,2,1,0:T(8,128)}, f32[64,8,128,128]{3,2,1,0:T(8,128)}, /*index=5*/s32[]{:T(128)}, s32[]{:T(128)}) while((s32[]{:T(128)}, f32[8,128,128]{1,2,0:T(8,128)S(1)}, s32[]{:T(128)}, f32[64,8,128,128]{3,2,1,0:T(8,128)}, ...), condition=%wide.region_5.6_spmd.clone, body=%wide.region_4.5_spmd.clone.sunk | while | flops 201850880 | bytes 5769315 | solution.py:32
  325.7 2.1 fusion.302
  329.1 2.1 fusion.302
  336.0 2.1 fusion.302
  342.9 2.1 fusion.302
  353.2 2.1 fusion.302
  360.1 2.1 fusion.302
  363.5 2.1 fusion.302
  370.4 2.1 fusion.302
  373.9 2.1 fusion.302
  391.1 2.1 fusion.302
  401.4 2.1 fusion.302
  408.3 2.1 fusion.302
  418.6 2.1 fusion.302
  422.0 2.1 fusion.302
  435.8 2.1 fusion.302
  439.2 2.1 fusion.302
  449.5 2.1 fusion.302
  456.4 2.1 fusion.302
  466.7 2.1 fusion.302
  483.9 2.1 fusion.302
  487.4 2.1 fusion.302
  494.2 2.1 fusion.302
  541.3 21.0 %while.37 = (s32[]{:T(128)}, f32[8,128,128]{2,1,0:T(8,128)S(1)}, f32[2,8,64,128]{3,2,1,0:T(8,128)S(1)}, f32[2,64,8]{1,2,0:T(8,128)S(1)}, f32[2,64,8]{1,2,0:T(8,1...) while((s32[]{:T(128)}, f32[8,128,128]{2,1,0:T(8,128)S(1)}, ...), condition=%wide.region_10.11_spmd, body=%wide.region_6.10_spmd.sunk | while | flops 756596736 | bytes 11366721 | solution.py:104
  563.1 4.1 fusion.42
  567.2 23.3 %reduce-scatter.2.cloned.1.call-done = f32[128,512]{1,0:T(8,128)} async-done(((f32[128,2048]{1,0:T(8,128)}), f32[128,512]{1,0:T(8,128)}) %reduce-scatter.2.cloned.1.call-update) | async-done | bytes 262160 | tf_op jit(solution)/shard_map/reduce_scatter | solution.py:182
  (398 shorter events, 214.8 us)
Async XLA Ops:
  6.5 34.1 %copy-start = (f32[128]{0:T(128)S(1)}, f32[128]{0:T(128)}, u32[]{:S(2)}) copy-start(f32[128]{0:T(128)} %param.29) | copy-start | bytes 1540
  6.5 175.5 %all-gather.5.cloned.1.call-start = ((), (), s32[]{:S(2)}) async-start(), calls=%async_computation.2 | async-start | bytes 34078720 | tf_op jit(solution)/shard_map/all_gather | solution.py:23
  8.7 8.3 %collective-permute-start = (bf16[3,2048]{1,0:T(4,128)(2,1)S(1)}, bf16[3,2048]{1,0:T(4,128)(2,1)S(1)}, u32[]{:S(2)}, u32[]{:S(2)}) collective-permute-start(bf16[3,2048]{1,0:T(4,128)(2,1)S(1)} %pad_maximum_fusion), channel_id=1, source_target_pairs={{0,4},{4,8},{8,12},{12,16},{16,20},{20,24},{24,28},{28,32},{32,36}... | collective-permute-start | bytes 36872 | tf_op jit(solution)/shard_map/ppermute | solution.py:18
  19.8 20.9 %copy-start.1 = (bf16[4,512]{1,0:T(4,128)(2,1)S(1)}, bf16[4,512]{1,0:T(4,128)(2,1)}, u32[]{:S(2)}) copy-start(bf16[4,512]{1,0:T(4,128)(2,1)} %param.22) | copy-start | bytes 12292
  39.6 284.8 %all-gather.7.cloned.1.call-start = ((), (), s32[]{:S(2)}) async-start(), calls=%async_computation.3 | async-start | bytes 34078720 | tf_op jit(solution)/shard_map/all_gather | solution.py:23
  40.3 550.2 %reduce-scatter.2.cloned.1.call-start = ((), (), s32[]{:S(2)}) async-start(), calls=%async_computation.1 | async-start | bytes 1310720 | tf_op jit(solution)/shard_map/reduce_scatter | solution.py:182
  541.2 21.9 %copy-start.2 = (bf16[128,1024]{1,0:T(8,128)(2,1)S(1)}, bf16[128,1024]{1,0:T(8,128)(2,1)}, u32[]{:S(2)}) copy-start(bf16[128,1024]{1,0:T(8,128)(2,1)} %param.30) | copy-start | bytes 786436
Sparse Core Ops, SparseCore 0:
  39.7 142.3 all-gather.4
  184.8 139.4 all-gather.6
  567.4 23.1 reduce-scatter.1
where the time goes:
time: 605 us; the launch traced here: 597 us
  waiting for transfers between devices  308 us (51%)
  matrix products  170 us (28%)
  local copies, waits for them, and re-layouts  88.2 us (15%)
  between operations  13.4 us (2%)
  other arithmetic  9.42 us (2%)
    all_gather x2, waiting for transfers between devices, carried_in(): pieces = jax.tree.map(lambda part: lax.all_gather(part, axis), value)  284 us
    dot_general x63, matrix products, compose(): jnp.einsum('hvj,hjk->hvk', earlier[1], later[0], precision=highest)  131 us
    dynamic_slice x126, local copies, waits for them, and re-layouts, lap(): longer = join(running, jax.tree.map(lambda part: part[position], pieces))  80.4 us
    reduce_scatter x1, waiting for transfers between devices, shards(): lax.psum_scatter(partial_terms, 'heads', scatter_dimension=1, tiled=True)  23.3 us
  transfers between devices with their start and end apart: 4, of which 3 were waited for; matrix products, arithmetic and copies ran while one was open for 1% of the time, Pallas kernels for 0%

commit v1 on v0

v1 whole, which is shorter than its diff:
```python
import functools

import jax
import jax.numpy as jnp
from jax import lax
from jax.experimental import pallas as pl
from jax.experimental.pallas import tpu as pltpu
from jax.sharding import PartitionSpec as P

DK = 128
DV = 128
TAIL = 16
MESH = pl.DeviceIdType.MESH
F32 = jnp.float32
BF16 = jnp.bfloat16
HIGHEST = lax.Precision.HIGHEST
KEY_GROUP = 2


def split(value):
    high = value.astype(BF16)
    return high, (value - high.astype(F32)).astype(BF16)


def mm(left, right):
    return jnp.dot(left, right, preferred_element_type=F32)


def one_pass(left, right):
    return mm(left.astype(BF16), right.astype(BF16))


def split_left(left, right):
    high, low = split(left)
    return mm(jnp.concatenate([high, low], axis=1), jnp.concatenate([right, right], axis=0))


def split_right(left, right):
    high, low = split(right)
    return mm(jnp.concatenate([left, left], axis=1), jnp.concatenate([high, low], axis=0))


def split_both(left, right):
    left_high, left_low = split(left)
    right_high, right_low = split(right)
    return mm(
        jnp.concatenate([left_high, left_low], axis=1),
        jnp.concatenate([right_high, right_high], axis=0),
    ) + mm(left_high, right_low)


def silu(value):
    return value * (1.0 / (1.0 + jnp.exp(-value)))


def three_parts(value):
    first = value.astype(BF16).astype(F32)
    second = (value - first).astype(BF16).astype(F32)
    return first, second, value - first - second


def pack_decay(decay, width):
    row = lax.broadcasted_iota(jnp.int32, (TAIL, width), 0)
    first, second, third = three_parts(decay)
    zero = jnp.zeros((TAIL, width), F32)
    block = jnp.where(row == 0, first, jnp.where(row == 1, second, jnp.where(row == 2, third, zero)))
    return block.astype(BF16)


def kernel(
    nx,
    ny,
    nz,
    q_hbm,
    k_hbm,
    v_hbm,
    z_hbm,
    w_hbm,
    a_ref,
    b_ref,
    alog_ref,
    bias_ref,
    gain_ref,
    cq_ref,
    ck_ref,
    cv_ref,
    out_ref,
    q_in,
    k_in,
    v_in,
    z_in,
    w_in,
    halo_q,
    halo_k,
    halo_v,
    ext,
    vc_all,
    kc_all,
    qc_all,
    up_out,
    up_in,
    pair,
    carry,
    pre_state,
    pre_map,
    pre_decay,
    sigma,
    down_out,
    down_in,
    reads,
    local,
    normed,
    rs_out,
    rs_in,
    load_sem,
    halo_send,
    halo_recv,
    up_send,
    up_recv,
    pair_sem,
    y_send,
    y_recv,
    down_send,
    down_recv,
    rs_send,
    rs_recv,
):
    rows = q_in.shape[0]
    key_heads = nz // 2
    ring = 2 * nz
    count = ny * ring
    me = lax.axis_index("ctx")
    x = lax.axis_index("heads")
    y = me // ring
    place = lax.rem(me, ring)
    z = place // 2
    core = lax.rem(place, 2)
    half = place // nz
    mine = lax.rem(place, nz)
    base = 2 * (z // 2)
    width = out_ref.shape[1]

    def head_of(slot):
        return lax.rem(base + slot, nz)

    loads = [
        pltpu.make_async_copy(source, target, load_sem.at[i])
        for i, (source, target) in enumerate(
            ((k_hbm, k_in), (v_hbm, v_in), (q_hbm, q_in), (z_hbm, z_in), (w_hbm, w_in))
        )
    ]
    for load in loads:
        load.start()

    barrier = pltpu.get_barrier_semaphore()

    def greet(ctx, heads):
        pl.semaphore_signal(barrier, inc=1, device_id=(ctx, heads), device_id_type=MESH)

    for step in range(1, ring):
        greet(y * ring + lax.rem(place + step, ring), x)
    for step in range(1, ny):
        greet(lax.rem(me + step * ring, count), x)
    for step in range(1, nx):
        greet(me, lax.rem(x + step, nx))
    over = jnp.logical_and(place == ring - 1, me < count - 1)
    under = jnp.logical_and(place == 0, me > 0)

    @pl.when(over)
    def _():
        greet(me + 1, x)

    @pl.when(under)
    def _():
        greet(me - 1, x)

    pl.semaphore_wait(
        barrier,
        (ring - 1) + (ny - 1) + (nx - 1) + over.astype(jnp.int32) + under.astype(jnp.int32),
    )

    def halo_copies(ctx):
        return [
            pltpu.make_async_remote_copy(
                src_ref=source.at[pl.ds(rows - TAIL, TAIL), :],
                dst_ref=target,
                send_sem=halo_send.at[i],
                recv_sem=halo_recv.at[i],
                device_id=(ctx, x),
                device_id_type=MESH,
            )
            for i, (source, target) in enumerate(
                ((k_hbm, halo_k), (v_hbm, halo_v), (q_hbm, halo_q))
            )
        ]

    following = lax.rem(me + 1, count)

    @pl.when(me < count - 1)
    def _():
        for copy in halo_copies(following):
            copy.start()

    @pl.when(me == 0)
    def _():
        halo_k[...] = jnp.zeros_like(halo_k)
        halo_v[...] = jnp.zeros_like(halo_v)
        halo_q[...] = jnp.zeros_like(halo_q)

    row = lax.broadcasted_iota(jnp.int32, (rows, rows), 0)
    col = lax.broadcasted_iota(jnp.int32, (rows, rows), 1)
    upto = row >= col
    strict = row > col
    apart = jnp.bitwise_xor(row, col)
    gate_in = a_ref[...] + bias_ref[...]
    softplus = jnp.maximum(gate_in, 0.0) + jnp.log1p(jnp.exp(-jnp.abs(gate_in)))
    logdecay = -jnp.exp(alog_ref[...]) * softplus
    beta = 1.0 / (1.0 + jnp.exp(-b_ref[...]))
    cumulative = jnp.dot(
        jnp.where(upto, 1.0, 0.0), logdecay, preferred_element_type=F32, precision=HIGHEST
    )
    from_head = lax.broadcasted_iota(jnp.int32, (nz, 128), 0)
    lane = lax.broadcasted_iota(jnp.int32, (nz, 128), 1)

    def placing(first):
        wanted = base + lane - first
        wanted = jnp.where(wanted >= nz, wanted - nz, wanted)
        inside = jnp.logical_and(lane >= first, lane < first + nz)
        return jnp.where(jnp.logical_and(inside, wanted == from_head), 1.0, 0.0)

    columns = jnp.dot(
        cumulative, placing(0), preferred_element_type=F32, precision=HIGHEST
    ) + jnp.dot(beta, placing(nz), preferred_element_type=F32, precision=HIGHEST)

    def conv(data, halo, taps_ref, start, size):
        cols = pl.ds(pl.multiple_of(start, 128), size)
        ext[0:8, 0:size] = halo[:, cols].astype(F32)[8:16]
        ext[8 : 8 + rows, 0:size] = data[:, cols].astype(F32)
        taps = taps_ref[:, cols].astype(F32)
        total = jnp.zeros((rows, size), F32)
        for j in range(4):
            total = total + taps[j : j + 1] * ext[5 + j : 5 + j + rows, 0:size]
        return silu(total).astype(BF16)

    def inverse_norm(block):
        entries = block.astype(F32)
        return lax.rsqrt(jnp.sum(entries * entries, axis=1, keepdims=True) + 1e-6)

    for load in loads[:3]:
        load.wait()

    @pl.when(me > 0)
    def _():
        for copy in halo_copies(following):
            copy.wait_recv()

    wide_lane = lax.broadcasted_iota(jnp.int32, (rows, 128), 1)
    for s in range(key_heads):
        kh = lax.rem(base // 2 + s, key_heads)
        kc_all[s] = conv(k_in, halo_k, ck_ref, kh * 128, 128)
        vc_all[s] = conv(v_in, halo_v, cv_ref, kh * 256, 256)
        qc_all[s] = conv(q_in, halo_q, cq_ref, kh * 128, 128)
        columns = jnp.where(wide_lane == 2 * nz + s, inverse_norm(kc_all[s]), columns)
        columns = jnp.where(
            wide_lane == 2 * nz + key_heads + s, inverse_norm(qc_all[s]) * DK**-0.5, columns
        )
    by_row = jnp.transpose(columns)

    def column(index):
        return columns[:, index : index + 1]

    def lane_row(index):
        return by_row[index : index + 1, :]

    def up_copy(slot):
        head = head_of(slot)
        return pltpu.make_async_remote_copy(
            src_ref=up_out.at[slot],
            dst_ref=up_in.at[mine],
            send_sem=up_send.at[slot],
            recv_sem=up_recv.at[mine],
            device_id=(y * ring + 2 * head + half, x),
            device_id_type=MESH,
        )

    def at_home(slot):
        return jnp.logical_and(head_of(slot) == z, half == core)

    for first in range(0, key_heads, KEY_GROUP):
        keys = range(first, first + KEY_GROUP)
        heads = [2 * s + p for s in keys for p in range(2)]
        gram, query_gram = {}, {}
        for s in keys:
            kc_t = kc_all[s]
            contract = (((1,), (1,)), ((), ()))
            gram[s] = lax.dot_general(kc_t, kc_t, contract, preferred_element_type=F32)
            query_gram[s] = lax.dot_general(
                qc_all[s], kc_t, contract, preferred_element_type=F32
            )
        within, lower, inverse = {}, {}, {}
        for h in heads:
            s = h // 2
            gaps = column(h) - lane_row(h)
            within[h] = jnp.exp(jnp.where(upto, gaps, -1e30)) * lane_row(2 * nz + s)
            scale = column(nz + h) * column(2 * nz + s)
            lower[h] = jnp.where(strict, scale * gram[s] * within[h], 0.0)
            inverse[h] = jnp.where(apart == 1, -lower[h], 0.0)
        level = 1
        while (1 << level) < rows:
            block, inner = {}, {}
            for h in heads:
                block[h] = jnp.where((apart >> level) == 1, lower[h], 0.0)
                inner[h] = block[h] + one_pass(block[h], inverse[h])
            for h in heads:
                inverse[h] = inverse[h] - inner[h] - one_pass(inverse[h], inner[h])
            level += 1
        values, maps = {}, {}
        for h in heads:
            s = h // 2
            solve = jnp.where(row == col, 1.0, inverse[h]) * lane_row(nz + h)
            values[h] = split_left(solve, vc_all[s, :, (h % 2) * 128 : (h % 2 + 1) * 128])
            key_solve = solve * (jnp.exp(lane_row(h)) * lane_row(2 * nz + s))
            maps[h] = split_left(key_solve, kc_all[s])
        for h in heads:
            s = h // 2
            last = columns[rows - 1 : rows, h : h + 1]
            tail = jnp.exp(last - column(h)) * column(2 * nz + s)
            both = jnp.concatenate([values[h] * tail, maps[h] * tail], axis=1)
            kc_t = jnp.transpose(kc_all[s].astype(F32)).astype(BF16)
            up_out[h, 0:DK, :] = split_right(kc_t, both).astype(BF16)
            up_out[h, DK:, :] = pack_decay(jnp.exp(last), DK + DV)

        for h in heads:
            home = at_home(h)

            @pl.when(home)
            def _(h=h):
                up_in[mine] = up_out[h]

            @pl.when(jnp.logical_not(home))
            def _(h=h):
                up_copy(h).start()

        for h in heads:
            s = h // 2
            attend = jnp.where(
                upto, query_gram[s] * within[h] * column(2 * nz + key_heads + s), 0.0
            )
            both = split_both(attend, jnp.concatenate([values[h], maps[h]], axis=1))
            local[h] = both[:, 0:DV]
            start = jnp.exp(column(h)) * column(2 * nz + key_heads + s)
            high, low = split(start * qc_all[s].astype(F32) - both[:, DV:])
            reads[h, :, 0:DK] = high
            reads[h, :, DK:] = low

    eye = lax.broadcasted_iota(jnp.int32, (DK, DK), 0) == lax.broadcasted_iota(
        jnp.int32, (DK, DK), 1
    )

    def decay_of(block):
        return jnp.sum(block.astype(F32), axis=0, keepdims=True)

    def up_wait(j):
        at = half_place(j)

        @pl.when(at != me)
        def _():
            pltpu.make_async_remote_copy(
                src_ref=up_out.at[0],
                dst_ref=up_in.at[j],
                send_sem=up_send.at[0],
                recv_sem=up_recv.at[j],
                device_id=(at, x),
                device_id_type=MESH,
            ).wait_recv()

    def half_place(j):
        return y * ring + core * nz + j

    def with_map(state, map_part, decay):
        return jnp.concatenate(
            [state.astype(F32), jnp.where(eye, decay, 0.0) - map_part.astype(F32)], axis=1
        )

    def compose(message, carried):
        decay = decay_of(message[DK:, :])
        fresh = jnp.concatenate(
            [message[0:DK, 0:DV].astype(F32), jnp.zeros((DK, DK), F32)], axis=1
        )
        return decay, decay * carried - mm(message[0:DK, DV:], carried.astype(BF16)) + fresh

    pre_state[0] = jnp.zeros((DK, DV), F32)
    pre_map[0] = jnp.zeros((DK, DK), BF16)
    pre_decay[0] = jnp.ones((8, 128), F32)
    total_decay = None
    carried = None
    for j in range(nz):
        up_wait(j)
        message = up_in[j]
        if j == 0:
            total_decay = decay_of(message[DK:, :])
            carried = with_map(message[0:DK, 0:DV], message[0:DK, DV:], total_decay[:, 0:DK])
        else:
            decay, carried = compose(message, carried)
            total_decay = total_decay * decay
        map_part = jnp.where(eye, total_decay[:, 0:DK], 0.0) - carried[:, DV:]
        if j < nz - 1:
            pre_state[j + 1] = carried[:, 0:DV]
            pre_map[j + 1] = map_part.astype(BF16)
            pre_decay[j + 1] = jnp.broadcast_to(total_decay[:, 0:128], (8, 128))

    def put_message(target, carried, total_decay):
        target[0:DK, 0:DV] = carried[:, 0:DV].astype(BF16)
        target[0:DK, DV:] = (
            jnp.where(eye, total_decay[:, 0:DK], 0.0) - carried[:, DV:]
        ).astype(BF16)
        target[DK:, :] = pack_decay(total_decay[:, 0:1], DK + DV)

    other = me + 1 - 2 * core
    put_message(pair.at[core], carried, total_decay)
    swap = pltpu.make_async_remote_copy(
        src_ref=pair.at[core],
        dst_ref=pair.at[core],
        send_sem=pair_sem.at[0],
        recv_sem=pair_sem.at[1],
        device_id=(other, x),
        device_id_type=MESH,
    )
    swap.start()
    pltpu.make_async_remote_copy(
        src_ref=pair.at[core],
        dst_ref=pair.at[1 - core],
        send_sem=pair_sem.at[0],
        recv_sem=pair_sem.at[1],
        device_id=(other, x),
        device_id_type=MESH,
    ).wait_recv()
    early = pair[0]
    early_decay = decay_of(early[DK:, :])
    decay, carried = compose(
        pair[1], with_map(early[0:DK, 0:DV], early[0:DK, DV:], early_decay[:, 0:DK])
    )
    put_message(carry.at[y], carried, early_decay * decay)

    def carry_copy(source, target_y):
        return pltpu.make_async_remote_copy(
            src_ref=carry.at[source],
            dst_ref=carry.at[source],
            send_sem=y_send.at[target_y],
            recv_sem=y_recv.at[source],
            device_id=(target_y * ring + place, x),
            device_id_type=MESH,
        )

    for later in range(1, ny):

        @pl.when(y < later)
        def _(later=later):
            carry_copy(y, later).start()

    sigma[...] = jnp.zeros((DK, DV), F32)

    def advance(message):
        state = sigma[...]
        sigma[...] = (
            decay_of(message[DK:, 0:DV]) * state
            - mm(message[0:DK, DV:], state.astype(BF16))
            + message[0:DK, 0:DV].astype(F32)
        )

    for earlier in range(ny - 1):

        @pl.when(y > earlier)
        def _(earlier=earlier):
            carry_copy(earlier, y).wait_recv()
            advance(carry[earlier])

    @pl.when(core == 1)
    def _():
        advance(pair[0])

    def down_copy(j):
        return pltpu.make_async_remote_copy(
            src_ref=down_out.at[j],
            dst_ref=down_in.at[z],
            send_sem=down_send.at[j],
            recv_sem=down_recv.at[z],
            device_id=(half_place(j), x),
            device_id_type=MESH,
        )

    start_state = sigma[...]
    rounded = start_state.astype(BF16)
    for j in range(nz):
        state = (
            pre_decay[j, 0:1, :] * start_state - mm(pre_map[j], rounded) + pre_state[j]
        ).astype(BF16)
        down_out[j] = state
        home = half_place(j) == me

        @pl.when(home)
        def _(j=j):
            down_in[z] = down_out[j]

        @pl.when(jnp.logical_not(home))
        def _(j=j):
            down_copy(j).start()

    for load in loads[3:]:
        load.wait()
    for h in range(nz):
        head = head_of(h)
        sender = y * ring + 2 * head + half

        @pl.when(sender != me)
        def _(head=head, sender=sender):
            pltpu.make_async_remote_copy(
                src_ref=down_out.at[0],
                dst_ref=down_in.at[head],
                send_sem=down_send.at[0],
                recv_sem=down_recv.at[head],
                device_id=(sender, x),
                device_id_type=MESH,
            ).wait_recv()

        state = down_in[head]
        core_out = mm(reads[h], jnp.concatenate([state, state], axis=0)) + local[h]
        cols = pl.ds(pl.multiple_of(head * DV, DV), DV)
        power = jnp.mean(core_out * core_out, axis=1, keepdims=True)
        gated = core_out * lax.rsqrt(power + 1e-6) * gain_ref[...]
        normed[:, cols] = (gated * silu(z_in[:, cols].astype(F32))).astype(BF16)

    def part(step):
        cols = pl.ds(pl.multiple_of(lax.rem(x + step, nx) * width, 128), width)
        return mm(normed[...], w_in[:, cols])

    def rs_copy(step):
        return pltpu.make_async_remote_copy(
            src_ref=rs_out.at[step - 1],
            dst_ref=rs_in.at[step - 1],
            send_sem=rs_send.at[step - 1],
            recv_sem=rs_recv.at[step - 1],
            device_id=(me, lax.rem(x + step, nx)),
            device_id_type=MESH,
        )

    order = sorted(range(1, nx), key=lambda step: -min(step, nx - step))
    for step in order:
        rs_out[step - 1] = part(step).astype(BF16)
        rs_copy(step).start()
    total = part(0)
    for step in reversed(order):
        rs_copy(step).wait_recv()
        total = total + rs_in[step - 1].astype(F32)
    out_ref[...] = total

    @pl.when(me < count - 1)
    def _():
        for copy in halo_copies(following):
            copy.wait_send()

    for slot in range(nz):

        @pl.when(jnp.logical_not(at_home(slot)))
        def _(slot=slot):
            up_copy(slot).wait_send()

        @pl.when(half_place(slot) != me)
        def _(slot=slot):
            down_copy(slot).wait_send()

    swap.wait_send()
    for later in range(1, ny):

        @pl.when(y < later)
        def _(later=later):
            carry_copy(y, later).wait_send()

    for step in order:
        rs_copy(step).wait_send()


def shards(
    q_in, k_in, v_in, conv_q, conv_k, conv_v, a_in, b_in, a_log, dt_bias, norm_weight, z_in, out_weight
):
    rows = q_in.shape[0]
    nz = v_in.shape[1] // DV
    nx = lax.axis_size("heads")
    ny = lax.axis_size("ctx") // (2 * nz)
    key_heads = nz // 2
    width = out_weight.shape[1] // nx
    hbm = pl.BlockSpec(memory_space=pl.ANY)
    vmem = pl.BlockSpec(memory_space=pltpu.VMEM)
    dma = pltpu.SemaphoreType.DMA
    message = (DK + TAIL, DK + DV)
    scratch = [
        pltpu.VMEM(q_in.shape, BF16),
        pltpu.VMEM(k_in.shape, BF16),
        pltpu.VMEM(v_in.shape, BF16),
        pltpu.VMEM(z_in.shape, BF16),
        pltpu.VMEM(out_weight.shape, BF16),
        pltpu.VMEM((TAIL, q_in.shape[1]), BF16),
        pltpu.VMEM((TAIL, k_in.shape[1]), BF16),
        pltpu.VMEM((TAIL, v_in.shape[1]), BF16),
        pltpu.VMEM((rows + 8, 2 * DV), F32),
        pltpu.VMEM((key_heads, rows, 2 * DV), BF16),
        pltpu.VMEM((key_heads, rows, DK), BF16),
        pltpu.VMEM((key_heads, rows, DK), BF16),
        pltpu.VMEM((nz,) + message, BF16),
        pltpu.VMEM((nz,) + message, BF16),
        pltpu.VMEM((2,) + message, BF16),
        pltpu.VMEM((ny,) + message, BF16),
        pltpu.VMEM((nz, DK, DV), F32),
        pltpu.VMEM((nz, DK, DK), BF16),
        pltpu.VMEM((nz, 8, 128), F32),
        pltpu.VMEM((DK, DV), F32),
        pltpu.VMEM((nz, DK, DV), BF16),
        pltpu.VMEM((nz, DK, DV), BF16),
        pltpu.VMEM((nz, rows, 2 * DK), BF16),
        pltpu.VMEM((nz, rows, DV), F32),
        pltpu.VMEM((rows, nz * DV), BF16),
        pltpu.VMEM((nx - 1, rows, width), BF16),
        pltpu.VMEM((nx - 1, rows, width), BF16),
        dma((5,)),
        dma((3,)),
        dma((3,)),
        dma((nz,)),
        dma((nz,)),
        dma((2,)),
        dma((ny,)),
        dma((ny,)),
        dma((nz,)),
        dma((nz,)),
        dma((nx - 1,)),
        dma((nx - 1,)),
    ]
    call = pl.pallas_call(
        functools.partial(kernel, nx, ny, nz),
        out_shape=jax.ShapeDtypeStruct((rows, width), F32),
        in_specs=[hbm] * 5 + [vmem] * 8,
        out_specs=vmem,
        scratch_shapes=scratch,
        compiler_params=pltpu.CompilerParams(
            collective_id=0, has_side_effects=True, vmem_limit_bytes=40 * 1024 * 1024
        ),
        cost_estimate=pl.CostEstimate(
            flops=2_000_000_000, bytes_accessed=6_000_000, transcendentals=1_000_000
        ),
    )
    return call(
        q_in,
        k_in,
        v_in,
        z_in,
        out_weight,
        a_in,
        b_in,
        a_log.reshape(1, nz),
        dt_bias.reshape(1, nz),
        norm_weight.reshape(1, DV),
        conv_q,
        conv_k,
        conv_v,
    )


def solution(mesh):
    in_specs = (
        P("ctx", "heads"),
        P("ctx", "heads"),
        P("ctx", "heads"),
        P(None, "heads"),
        P(None, "heads"),
        P(None, "heads"),
        P("ctx", "heads"),
        P("ctx", "heads"),
        P("heads"),
        P("heads"),
        P(),
        P("ctx", "heads"),
        P("heads", None),
    )
    out_specs = P("ctx", "heads")
    return jax.shard_map(shards, mesh=mesh, in_specs=in_specs, out_specs=out_specs, check_vma=False)
```

time: 605 us -> 68.6 us (0.11); the launches traced: 597 us -> 68.2 us
  waiting for transfers between devices: 308 us -> 0 us
  matrix products: 170 us -> 0 us
  local copies, waits for them, and re-layouts: 88.2 us -> 12.2 us
  Pallas kernels: 0 us -> 55.9 us
  between operations: 13.4 us -> 0.03 us
  other arithmetic: 9.42 us -> 0 us
    all_gather x2 -> x0, waiting for transfers between devices: 284 us -> none  [carried_in(): pieces = jax.tree.map(lambda part: lax.all_gather(part, axis), value)]
    dot_general x126 -> x0, matrix products: 170 us -> none  [the longest x63 131 us: compose(): jnp.einsum('hvj,hjk->hvk', earlier[1], later[0], precision=highest)]
    dynamic_slice x128 -> x0, local copies, waits for them, and re-layouts: 80.5 us -> none  [the longest x126 80.4 us: lap(): longer = join(running, jax.tree.map(lambda part: part[position], pieces))]
    pallas_call x0 -> x1, Pallas kernels: none -> 55.9 us  [shards(): call(q_in, k_in, v_in, z_in, out_weight, a_in, b_in, a_log.reshape(1, nz)...]
    reduce_scatter x1 -> x0, waiting for transfers between devices: 23.3 us -> none  [shards(): lax.psum_scatter(partial_terms, 'heads', scatter_dimension=1, tiled=True)]
    unnamed x7 -> x25, local copies, waits for them, and re-layouts: 0.06 us -> 12.2 us
  transfers between devices with their start and end apart: 4 -> 0, of which waited for: 3 -> 0; matrix products, arithmetic and copies ran while one was open for 1% -> 0% of each run, Pallas kernels for 0% -> 0%
where the time goes in v1:
time: 68.6 us; the launch traced here: 68.2 us
  Pallas kernels  55.9 us (81%)
  local copies, waits for them, and re-layouts  12.2 us (18%)
    pallas_call x1, Pallas kernels, shards(): call(q_in, k_in, v_in, z_in, out_weight, a_in, b_in, a_log.reshape(1, nz)...  55.9 us
    unnamed x25, local copies, waits for them, and re-layouts  12.2 us

profile of v1, /device:TPU:25, one launch (start us, length us, event | category | flops | bytes accessed | tf_op | source)
XLA Modules:
  0.0 68.2 jit_solution(7524229850865772977)
XLA Ops:
  0.0 0.8 %copy.14.a_ref = f32[128,8]{1,0:T(8,128)S(1)} copy(f32[128,8]{0,1:T(8,128)} %param.19) | data formatting | bytes 8192 | tf_op args[6]
  0.8 0.8 %copy.15.b_ref = f32[128,8]{1,0:T(8,128)S(1)} copy(f32[128,8]{0,1:T(8,128)} %param.20) | data formatting | bytes 8192 | tf_op args[7]
  1.6 0.0 copy-start
  1.6 2.2 %copy-done = bf16[1024,2048]{1,0:T(8,128)(2,1)S(1)} copy-done((bf16[1024,2048]{1,0:T(8,128)(2,1)S(1)}, bf16[1024,2048]{1,0:T(8,128)(2,1)}, u32[]{:S(2)}) %copy-start) | copy-done | bytes 4194328
  3.8 0.0 copy-start.1
  3.8 0.9 %copy-done.1 = bf16[128,1024]{1,0:T(8,128)(2,1)S(1)} copy-done((bf16[128,1024]{1,0:T(8,128)(2,1)S(1)}, bf16[128,1024]{1,0:T(8,128)(2,1)}, u32[]{:S(2)}) %copy-start.1) | copy-done | bytes 262168
  4.7 0.0 copy-start.2
  4.7 0.9 %copy-done.2 = bf16[128,1024]{1,0:T(8,128)(2,1)S(1)} copy-done((bf16[128,1024]{1,0:T(8,128)(2,1)S(1)}, bf16[128,1024]{1,0:T(8,128)(2,1)}, u32[]{:S(2)}) %copy-start.2) | copy-done | bytes 262168
  5.7 0.0 copy-start.3
  5.7 0.9 %copy-done.3 = bf16[128,512]{1,0:T(8,128)(2,1)S(1)} copy-done((bf16[128,512]{1,0:T(8,128)(2,1)S(1)}, bf16[128,512]{1,0:T(8,128)(2,1)}, u32[]{:S(2)}) %copy-start.3) | copy-done | bytes 131096
  6.6 0.0 copy-start.4
  6.6 0.9 %copy-done.4 = bf16[128,512]{1,0:T(8,128)(2,1)S(1)} copy-done((bf16[128,512]{1,0:T(8,128)(2,1)S(1)}, bf16[128,512]{1,0:T(8,128)(2,1)}, u32[]{:S(2)}) %copy-start.4) | copy-done | bytes 131096
  7.5 0.0 copy-start.5
  7.5 0.7 %copy-done.5 = bf16[4,1024]{1,0:T(4,128)(2,1)S(1)} copy-done((bf16[4,1024]{1,0:T(4,128)(2,1)S(1)}, bf16[4,1024]{1,0:T(4,128)(2,1)}, u32[]{:S(2)}) %copy-start.5) | copy-done | bytes 8216
  8.2 0.0 copy-start.6
  8.2 0.7 %copy-done.6 = bf16[4,512]{1,0:T(4,128)(2,1)S(1)} copy-done((bf16[4,512]{1,0:T(4,128)(2,1)S(1)}, bf16[4,512]{1,0:T(4,128)(2,1)}, u32[]{:S(2)}) %copy-start.6) | copy-done | bytes 4120
  8.9 0.0 copy-start.7
  8.9 0.7 %copy-done.7 = bf16[4,512]{1,0:T(4,128)(2,1)S(1)} copy-done((bf16[4,512]{1,0:T(4,128)(2,1)S(1)}, bf16[4,512]{1,0:T(4,128)(2,1)}, u32[]{:S(2)}) %copy-start.7) | copy-done | bytes 4120
  9.5 0.0 copy-start.8
  9.5 0.7 copy-done.8
  10.2 0.0 copy-start.9
  10.2 0.7 copy-done.9
  10.9 0.0 copy-start.10
  10.9 0.7 copy-done.10
  11.5 55.9 %shard_map.127 = f32[128,512]{1,0:T(8,128)S(1)} custom-call(bf16[128,512]{1,0:T(8,128)(2,1)S(1)} %copy-done.3, bf16[128,512]{1,0:T(8,128)(2,1)S(1)} %copy-done.4, bf16[128,1024]{1,0:T(8,128)(2,1)S(1)} %copy-done.1, bf16[128,1024]{1,0:T(8,128)(2,1)S(1)} %copy-done.2, bf16[1024,2048]{1,0:T(8,128)(2,1)S(1)} %copy-done, f32[128,8]{1,0:T(8,128)S(1)} %copy.14.a_ref, ...), custom_call_target="tpu_custom_call" | custom-call | flops 2000000000 | bytes 6000000 | tf_op jit(solution)/shard_map/pallas_call | solution.py:650
  67.5 0.7 %copy.17 = f32[128,512]{1,0:T(8,128)} copy(f32[128,512]{1,0:T(8,128)S(1)} %shard_map.127) | data formatting | bytes 524288
Async XLA Ops:
  1.6 2.2 %copy-start = (bf16[1024,2048]{1,0:T(8,128)(2,1)S(1)}, bf16[1024,2048]{1,0:T(8,128)(2,1)}, u32[]{:S(2)}) copy-start(bf16[1024,2048]{1,0:T(8,128)(2,1)} %w_hbm.1) | copy-start | bytes 12582916
  3.8 0.9 %copy-start.1 = (bf16[128,1024]{1,0:T(8,128)(2,1)S(1)}, bf16[128,1024]{1,0:T(8,128)(2,1)}, u32[]{:S(2)}) copy-start(bf16[128,1024]{1,0:T(8,128)(2,1)} %v_hbm.1) | copy-start | bytes 786436
  4.7 0.9 %copy-start.2 = (bf16[128,1024]{1,0:T(8,128)(2,1)S(1)}, bf16[128,1024]{1,0:T(8,128)(2,1)}, u32[]{:S(2)}) copy-start(bf16[128,1024]{1,0:T(8,128)(2,1)} %z_hbm.1) | copy-start | bytes 786436
  5.7 0.9 %copy-start.3 = (bf16[128,512]{1,0:T(8,128)(2,1)S(1)}, bf16[128,512]{1,0:T(8,128)(2,1)}, u32[]{:S(2)}) copy-start(bf16[128,512]{1,0:T(8,128)(2,1)} %q_hbm.1) | copy-start | bytes 393220
  6.6 0.9 %copy-start.4 = (bf16[128,512]{1,0:T(8,128)(2,1)S(1)}, bf16[128,512]{1,0:T(8,128)(2,1)}, u32[]{:S(2)}) copy-start(bf16[128,512]{1,0:T(8,128)(2,1)} %k_hbm.1) | copy-start | bytes 393220
  7.5 0.7 %copy-start.5 = (bf16[4,1024]{1,0:T(4,128)(2,1)S(1)}, bf16[4,1024]{1,0:T(4,128)(2,1)}, u32[]{:S(2)}) copy-start(bf16[4,1024]{1,0:T(4,128)(2,1)} %cv_ref.1) | copy-start | bytes 24580
  8.2 0.7 %copy-start.6 = (bf16[4,512]{1,0:T(4,128)(2,1)S(1)}, bf16[4,512]{1,0:T(4,128)(2,1)}, u32[]{:S(2)}) copy-start(bf16[4,512]{1,0:T(4,128)(2,1)} %cq_ref.1) | copy-start | bytes 12292
  8.9 0.7 %copy-start.7 = (bf16[4,512]{1,0:T(4,128)(2,1)S(1)}, bf16[4,512]{1,0:T(4,128)(2,1)}, u32[]{:S(2)}) copy-start(bf16[4,512]{1,0:T(4,128)(2,1)} %ck_ref.1) | copy-start | bytes 12292
  9.5 0.7 copy-start.8
  10.2 0.7 copy-start.9
  10.9 0.7 copy-start.10

commit v2 on v1

v2 whole, which is shorter than its diff:
```python
import functools

import jax
import jax.numpy as jnp
from jax import lax
from jax.experimental import pallas as pl
from jax.experimental.pallas import tpu as pltpu
from jax.sharding import PartitionSpec as P

DK = 128
DV = 128
TAIL = 16
MESH = pl.DeviceIdType.MESH
F32 = jnp.float32
BF16 = jnp.bfloat16
HIGHEST = lax.Precision.HIGHEST


def split(value):
    high = value.astype(BF16)
    return high, (value - high.astype(F32)).astype(BF16)


def mm(left, right):
    return jnp.dot(left, right, preferred_element_type=F32)


def one_pass(left, right):
    return mm(left.astype(BF16), right.astype(BF16))


def split_left(left, right):
    high, low = split(left)
    return mm(jnp.concatenate([high, low], axis=1), jnp.concatenate([right, right], axis=0))


def split_right(left, right):
    high, low = split(right)
    return mm(jnp.concatenate([left, left], axis=1), jnp.concatenate([high, low], axis=0))


def split_both(left, right):
    left_high, left_low = split(left)
    right_high, right_low = split(right)
    return mm(
        jnp.concatenate([left_high, left_low], axis=1),
        jnp.concatenate([right_high, right_high], axis=0),
    ) + mm(left_high, right_low)


def silu(value):
    return value * (1.0 / (1.0 + jnp.exp(-value)))


def three_parts(value):
    first = value.astype(BF16).astype(F32)
    second = (value - first).astype(BF16).astype(F32)
    return first, second, value - first - second


def pack_decay(decay, width):
    row = lax.broadcasted_iota(jnp.int32, (TAIL, width), 0)
    first, second, third = three_parts(decay)
    zero = jnp.zeros((TAIL, width), F32)
    block = jnp.where(row == 0, first, jnp.where(row == 1, second, jnp.where(row == 2, third, zero)))
    return block.astype(BF16)


def kernel(
    nx,
    ny,
    nz,
    q_hbm,
    k_hbm,
    v_hbm,
    z_hbm,
    w_hbm,
    a_hbm,
    b_hbm,
    alog_hbm,
    bias_hbm,
    gain_hbm,
    cq_hbm,
    ck_hbm,
    cv_hbm,
    out_ref,
    q_in,
    k_in,
    v_in,
    z_in,
    w_in,
    a_ref,
    b_ref,
    alog_ref,
    bias_ref,
    gain_ref,
    cq_ref,
    ck_ref,
    cv_ref,
    halo_q,
    halo_k,
    halo_v,
    ext,
    vc_all,
    kc_all,
    qc_all,
    chunk_maps,
    up_out,
    up_in,
    carry,
    pre_state,
    pre_map,
    pre_decay,
    sigma,
    down_out,
    down_in,
    reads,
    local,
    normed,
    rs_out,
    rs_in,
    load_sem,
    halo_send,
    halo_recv,
    chip_send,
    chip_recv,
    up_send,
    up_recv,
    y_send,
    y_recv,
    down_send,
    down_recv,
    pass_send,
    pass_recv,
    rs_send,
    rs_recv,
):
    rows = q_in.shape[0]
    key_heads = nz // 2
    ring = 2 * nz
    count = ny * ring
    me = lax.axis_index("ctx")
    x = lax.axis_index("heads")
    y = me // ring
    place = lax.rem(me, ring)
    z = place // 2
    core = lax.rem(place, 2)
    partner = me + 1 - 2 * core
    width = out_ref.shape[1]

    def first_head(chip):
        return lax.rem(2 * (chip // 2 + 1), nz)

    base = first_head(z)
    own_slots = [2 * (core + 2 * g) + p for g in range(nz // 4) for p in range(2)]
    other_slots = [2 * (1 - core + 2 * g) + p for g in range(nz // 4) for p in range(2)]

    def head_of(slot):
        return lax.rem(base + slot, nz)

    def owner_of(slot):
        return y * ring + 2 * head_of(slot)

    loads = [
        pltpu.make_async_copy(source, target, load_sem.at[i])
        for i, (source, target) in enumerate(
            (
                (a_hbm, a_ref),
                (b_hbm, b_ref),
                (alog_hbm, alog_ref),
                (bias_hbm, bias_ref),
                (ck_hbm, ck_ref),
                (cv_hbm, cv_ref),
                (cq_hbm, cq_ref),
                (k_hbm, k_in),
                (v_hbm, v_in),
                (q_hbm, q_in),
                (gain_hbm, gain_ref),
                (z_hbm, z_in),
                (w_hbm, w_in),
            )
        )
    ]
    for load in loads:
        load.start()

    barrier = pltpu.get_barrier_semaphore()

    def greet(ctx, heads):
        pl.semaphore_signal(barrier, inc=1, device_id=(ctx, heads), device_id_type=MESH)

    for step in range(1, ring):
        greet(y * ring + lax.rem(place + step, ring), x)
    for step in range(1, ny):
        greet(lax.rem(me + step * ring, count), x)
    for step in range(1, nx):
        greet(me, lax.rem(x + step, nx))
    over = jnp.logical_and(place == ring - 1, me < count - 1)
    under = jnp.logical_and(place == 0, me > 0)

    @pl.when(over)
    def _():
        greet(me + 1, x)

    @pl.when(under)
    def _():
        greet(me - 1, x)

    pl.semaphore_wait(
        barrier,
        (ring - 1) + (ny - 1) + (nx - 1) + over.astype(jnp.int32) + under.astype(jnp.int32),
    )

    def halo_copies(ctx):
        return [
            pltpu.make_async_remote_copy(
                src_ref=source.at[pl.ds(rows - TAIL, TAIL), :],
                dst_ref=target,
                send_sem=halo_send.at[i],
                recv_sem=halo_recv.at[i],
                device_id=(ctx, x),
                device_id_type=MESH,
            )
            for i, (source, target) in enumerate(
                ((k_hbm, halo_k), (v_hbm, halo_v), (q_hbm, halo_q))
            )
        ]

    following = lax.rem(me + 1, count)

    @pl.when(me < count - 1)
    def _():
        for copy in halo_copies(following):
            copy.start()

    @pl.when(me == 0)
    def _():
        halo_k[...] = jnp.zeros_like(halo_k)
        halo_v[...] = jnp.zeros_like(halo_v)
        halo_q[...] = jnp.zeros_like(halo_q)

    row = lax.broadcasted_iota(jnp.int32, (rows, rows), 0)
    col = lax.broadcasted_iota(jnp.int32, (rows, rows), 1)
    upto = row >= col
    strict = row > col
    apart = jnp.bitwise_xor(row, col)
    for load in loads[:4]:
        load.wait()
    head_row = lax.broadcasted_iota(jnp.int32, (nz, nz), 0)
    head_lane = lax.broadcasted_iota(jnp.int32, (nz, nz), 1)

    def per_head(values):
        return jnp.sum(jnp.where(head_row == head_lane, values, 0.0), axis=1, keepdims=True)

    gate_in = a_ref[...] + per_head(bias_ref[...])
    softplus = jnp.maximum(gate_in, 0.0) + jnp.log1p(jnp.exp(-jnp.abs(gate_in)))
    logdecay = -jnp.exp(per_head(alog_ref[...])) * softplus
    beta = 1.0 / (1.0 + jnp.exp(-b_ref[...]))
    cumulative = jnp.dot(
        logdecay, jnp.where(row <= col, 1.0, 0.0), preferred_element_type=F32, precision=HIGHEST
    )
    slot = lax.broadcasted_iota(jnp.int32, (128, nz), 0)
    from_head = lax.broadcasted_iota(jnp.int32, (128, nz), 1)

    def placing(first):
        wanted = base + slot - first
        wanted = jnp.where(wanted >= nz, wanted - nz, wanted)
        inside = jnp.logical_and(slot >= first, slot < first + nz)
        return jnp.where(jnp.logical_and(inside, wanted == from_head), 1.0, 0.0)

    columns = jnp.transpose(
        jnp.dot(placing(0), cumulative, preferred_element_type=F32, precision=HIGHEST)
        + jnp.dot(placing(nz), beta, preferred_element_type=F32, precision=HIGHEST)
    )

    def conv(before, data, taps_ref, start, size, count_rows):
        cols = pl.ds(pl.multiple_of(start, 128), size)
        ext[0:8, 0:size] = before
        ext[8 : 8 + count_rows, 0:size] = data[0:count_rows, cols].astype(F32)
        taps = taps_ref[:, cols].astype(F32)
        total = jnp.zeros((count_rows, size), F32)
        for j in range(4):
            total = total + taps[j : j + 1] * ext[5 + j : 5 + j + count_rows, 0:size]
        return silu(total).astype(BF16)

    def inverse_norm(block):
        entries = block.astype(F32)
        return lax.rsqrt(jnp.sum(entries * entries, axis=1, keepdims=True) + 1e-6)

    for load in loads[4:10]:
        load.wait()

    streams = (
        (k_in, halo_k, ck_ref, kc_all, DK),
        (v_in, halo_v, cv_ref, vc_all, 2 * DV),
        (q_in, halo_q, cq_ref, qc_all, DK),
    )
    for s in range(key_heads):
        kh = lax.rem(base // 2 + s, key_heads)
        for data, halo, taps_ref, result, size in streams:
            before = jnp.zeros((8, size), F32)
            result[s] = conv(before, data, taps_ref, kh * size, size, rows)

    @pl.when(me > 0)
    def _():
        for copy in halo_copies(following):
            copy.wait_recv()

    wide_lane = lax.broadcasted_iota(jnp.int32, (rows, 128), 1)
    for s in range(key_heads):
        kh = lax.rem(base // 2 + s, key_heads)
        for data, halo, taps_ref, result, size in streams:
            cols = pl.ds(pl.multiple_of(kh * size, 128), size)
            before = halo[:, cols].astype(F32)[8:16]
            result[s, 0:TAIL, :] = conv(before, data, taps_ref, kh * size, size, TAIL)
        columns = jnp.where(wide_lane == 2 * nz + s, inverse_norm(kc_all[s]), columns)
        columns = jnp.where(
            wide_lane == 2 * nz + key_heads + s, inverse_norm(qc_all[s]) * DK**-0.5, columns
        )
    by_row = jnp.transpose(columns)

    def column(index):
        return columns[:, index : index + 1]

    def lane_row(index):
        return by_row[index : index + 1, :]

    def chip_copy(slot):
        return pltpu.make_async_remote_copy(
            src_ref=chunk_maps.at[core, slot],
            dst_ref=chunk_maps.at[core, slot],
            send_sem=chip_send.at[slot],
            recv_sem=chip_recv.at[slot],
            device_id=(partner, x),
            device_id_type=MESH,
        )

    def chip_wait(slot):
        pltpu.make_async_remote_copy(
            src_ref=chunk_maps.at[core, slot],
            dst_ref=chunk_maps.at[1 - core, slot],
            send_sem=chip_send.at[slot],
            recv_sem=chip_recv.at[slot],
            device_id=(partner, x),
            device_id_type=MESH,
        ).wait_recv()

    def up_copy(index, slot):
        return pltpu.make_async_remote_copy(
            src_ref=up_out.at[index],
            dst_ref=up_in.at[z],
            send_sem=up_send.at[index],
            recv_sem=up_recv.at[z],
            device_id=(owner_of(slot), x),
            device_id_type=MESH,
        )

    keys = range(key_heads)
    heads = range(nz)
    gram, query_gram = {}, {}
    for s in keys:
        kc_t = kc_all[s]
        contract = (((1,), (1,)), ((), ()))
        gram[s] = lax.dot_general(kc_t, kc_t, contract, preferred_element_type=F32)
        query_gram[s] = lax.dot_general(
            qc_all[s], kc_t, contract, preferred_element_type=F32
        )
    within, lower, inverse = {}, {}, {}
    for h in heads:
        s = h // 2
        gaps = column(h) - lane_row(h)
        within[h] = jnp.exp(jnp.where(upto, gaps, -1e30)) * lane_row(2 * nz + s)
        scale = column(nz + h) * column(2 * nz + s)
        lower[h] = jnp.where(strict, scale * gram[s] * within[h], 0.0)
        inverse[h] = jnp.where(apart == 1, -lower[h], 0.0)
    level = 1
    while (1 << level) < rows:
        block, inner = {}, {}
        for h in heads:
            block[h] = jnp.where((apart >> level) == 1, lower[h], 0.0)
            inner[h] = block[h] + one_pass(block[h], inverse[h])
        for h in heads:
            inverse[h] = inverse[h] - inner[h] - one_pass(inverse[h], inner[h])
        level += 1
    values, maps = {}, {}
    for h in heads:
        s = h // 2
        solve = jnp.where(row == col, 1.0, inverse[h]) * lane_row(nz + h)
        values[h] = split_left(solve, vc_all[s, :, (h % 2) * 128 : (h % 2 + 1) * 128])
        key_solve = solve * (jnp.exp(lane_row(h)) * lane_row(2 * nz + s))
        maps[h] = split_left(key_solve, kc_all[s])
    for h in heads:
        s = h // 2
        last = columns[rows - 1 : rows, h : h + 1]
        tail = jnp.exp(last - column(h)) * column(2 * nz + s)
        both = jnp.concatenate([values[h] * tail, maps[h] * tail], axis=1)
        kc_t = jnp.transpose(kc_all[s].astype(F32)).astype(BF16)
        chunk_maps[core, h, 0:DK, :] = split_right(kc_t, both).astype(BF16)
        chunk_maps[core, h, DK:, :] = pack_decay(jnp.exp(last), DK + DV)
    for h in heads:
        chip_copy(h).start()

    def read_out(h):
        s = h // 2
        attend = jnp.where(
            upto, query_gram[s] * within[h] * column(2 * nz + key_heads + s), 0.0
        )
        both = split_both(attend, jnp.concatenate([values[h], maps[h]], axis=1))
        local[h] = both[:, 0:DV]
        start = jnp.exp(column(h)) * column(2 * nz + key_heads + s)
        high, low = split(start * qc_all[s].astype(F32) - both[:, DV:])
        reads[h, :, 0:DK] = high
        reads[h, :, DK:] = low

    eye = lax.broadcasted_iota(jnp.int32, (DK, DK), 0) == lax.broadcasted_iota(
        jnp.int32, (DK, DK), 1
    )

    def decay_of(block):
        return jnp.sum(block.astype(F32), axis=0, keepdims=True)

    def with_map(message, decay):
        map_part = jnp.where(eye, decay[:, 0:DK], 0.0) - message[0:DK, DV:].astype(F32)
        return jnp.concatenate([message[0:DK, 0:DV].astype(F32), map_part], axis=1)

    def compose(message, carried):
        decay = decay_of(message[DK:, :])
        fresh = jnp.concatenate(
            [message[0:DK, 0:DV].astype(F32), jnp.zeros((DK, DK), F32)], axis=1
        )
        return decay, decay * carried - mm(message[0:DK, DV:], carried.astype(BF16)) + fresh

    def put_message(target, carried, total_decay):
        target[0:DK, 0:DV] = carried[:, 0:DV].astype(BF16)
        target[0:DK, DV:] = (
            jnp.where(eye, total_decay[:, 0:DK], 0.0) - carried[:, DV:]
        ).astype(BF16)
        target[DK:, :] = pack_decay(total_decay[:, 0:1], DK + DV)

    for h in heads[: nz // 2]:
        read_out(h)
    for slot in own_slots:
        chip_wait(slot)
    joined = []
    for slot in own_slots:
        early, late = chunk_maps[0, slot], chunk_maps[1, slot]
        early_decay = decay_of(early[DK:, :])
        decay, carried = compose(late, with_map(early, early_decay))
        joined.append((carried, early_decay * decay))
    for index, slot in enumerate(own_slots):
        put_message(up_out.at[index], *joined[index])
        up_copy(index, slot).start()
    for h in heads[nz // 2 :]:
        read_out(h)

    for slot in other_slots:
        chip_wait(slot)

    @pl.when(core == 1)
    def _():
        for h in heads:
            early = chunk_maps[0, h]
            decay = decay_of(early[DK:, 0:DK])
            moved = mm(reads[h], jnp.concatenate([early[0:DK, :], early[0:DK, :]], axis=0))
            local[h] = local[h] + moved[:, 0:DV]
            whole = reads[h, :, 0:DK].astype(F32) + reads[h, :, DK:].astype(F32)
            high, low = split(decay * whole - moved[:, DV:])
            reads[h, :, 0:DK] = high
            reads[h, :, DK:] = low

    def carry_copy(source, target_y):
        return pltpu.make_async_remote_copy(
            src_ref=carry.at[source],
            dst_ref=carry.at[source],
            send_sem=y_send.at[target_y],
            recv_sem=y_recv.at[source],
            device_id=(target_y * ring + place, x),
            device_id_type=MESH,
        )

    def down_copy(chip):
        slot = lax.rem(z - first_head(chip) + nz, nz)
        return pltpu.make_async_remote_copy(
            src_ref=down_out.at[chip],
            dst_ref=down_in.at[slot],
            send_sem=down_send.at[chip],
            recv_sem=down_recv.at[slot],
            device_id=(y * ring + 2 * chip + lax.rem(slot // 2, 2), x),
            device_id_type=MESH,
        )

    @pl.when(core == 0)
    def _():
        pre_state[0] = jnp.zeros((DK, DV), F32)
        pre_map[0] = jnp.zeros((DK, DK), BF16)
        pre_decay[0] = jnp.ones((8, 128), F32)
        total_decay = None
        carried = None
        for j in range(nz):
            pltpu.make_async_remote_copy(
                src_ref=up_out.at[0],
                dst_ref=up_in.at[j],
                send_sem=up_send.at[0],
                recv_sem=up_recv.at[j],
                device_id=(partner, x),
                device_id_type=MESH,
            ).wait_recv()
            message = up_in[j]
            if j == 0:
                total_decay = decay_of(message[DK:, :])
                carried = with_map(message, total_decay)
            else:
                decay, carried = compose(message, carried)
                total_decay = total_decay * decay
            if j < nz - 1:
                pre_state[j + 1] = carried[:, 0:DV]
                pre_map[j + 1] = (
                    jnp.where(eye, total_decay[:, 0:DK], 0.0) - carried[:, DV:]
                ).astype(BF16)
                pre_decay[j + 1] = jnp.broadcast_to(total_decay[:, 0:128], (8, 128))
        put_message(carry.at[y], carried, total_decay)

        for later in range(1, ny):

            @pl.when(y < later)
            def _(later=later):
                carry_copy(y, later).start()

        sigma[...] = jnp.zeros((DK, DV), F32)
        for earlier in range(ny - 1):

            @pl.when(y > earlier)
            def _(earlier=earlier):
                carry_copy(earlier, y).wait_recv()
                message = carry[earlier]
                state = sigma[...]
                sigma[...] = (
                    decay_of(message[DK:, 0:DV]) * state
                    - mm(message[0:DK, DV:], state.astype(BF16))
                    + message[0:DK, 0:DV].astype(F32)
                )

        start_state = sigma[...]
        rounded = start_state.astype(BF16)
        for offset in sorted(range(nz), key=lambda offset: -min(offset, nz - offset)):
            chip = lax.rem(z + offset, nz)
            down_out[chip] = (
                pre_decay[chip, 0:1, :] * start_state - mm(pre_map[chip], rounded) + pre_state[chip]
            ).astype(BF16)
            down_copy(chip).start()

    def pass_copy(slot):
        return pltpu.make_async_remote_copy(
            src_ref=down_in.at[slot],
            dst_ref=down_in.at[slot],
            send_sem=pass_send.at[slot],
            recv_sem=pass_recv.at[slot],
            device_id=(partner, x),
            device_id_type=MESH,
        )

    for load in loads[10:]:
        load.wait()
    nearest = own_slots[len(own_slots) // 2 :] + own_slots[: len(own_slots) // 2]
    for slot in nearest:
        pltpu.make_async_remote_copy(
            src_ref=down_out.at[0],
            dst_ref=down_in.at[slot],
            send_sem=down_send.at[0],
            recv_sem=down_recv.at[slot],
            device_id=(owner_of(slot), x),
            device_id_type=MESH,
        ).wait_recv()
        pass_copy(slot).start()

    def finish(slots):
        cores = []
        for slot in slots:
            state = down_in[slot]
            cores.append(mm(reads[slot], jnp.concatenate([state, state], axis=0)) + local[slot])
        for slot, core_out in zip(slots, cores):
            head = head_of(slot)
            cols = pl.ds(pl.multiple_of(head * DV, DV), DV)
            power = jnp.mean(core_out * core_out, axis=1, keepdims=True)
            gated = core_out * lax.rsqrt(power + 1e-6) * gain_ref[...]
            normed[:, cols] = (gated * silu(z_in[:, cols].astype(F32))).astype(BF16)

    finish(nearest)
    for slot in other_slots:
        pass_copy(slot).wait_recv()
    finish(other_slots)

    def part(step):
        cols = pl.ds(pl.multiple_of(lax.rem(x + step, nx) * width, 128), width)
        return mm(normed[...], w_in[:, cols])

    def rs_copy(step):
        return pltpu.make_async_remote_copy(
            src_ref=rs_out.at[step - 1],
            dst_ref=rs_in.at[step - 1],
            send_sem=rs_send.at[step - 1],
            recv_sem=rs_recv.at[step - 1],
            device_id=(me, lax.rem(x + step, nx)),
            device_id_type=MESH,
        )

    order = sorted(range(1, nx), key=lambda step: -min(step, nx - step))
    for step in order:
        rs_out[step - 1] = part(step).astype(BF16)
        rs_copy(step).start()
    total = part(0)
    for step in reversed(order):
        rs_copy(step).wait_recv()
        total = total + rs_in[step - 1].astype(F32)
    out_ref[...] = total

    @pl.when(me < count - 1)
    def _():
        for copy in halo_copies(following):
            copy.wait_send()

    for h in heads:
        chip_copy(h).wait_send()
    for index, slot in enumerate(own_slots):
        up_copy(index, slot).wait_send()
        pass_copy(slot).wait_send()

    @pl.when(core == 0)
    def _():
        for chip in range(nz):
            down_copy(chip).wait_send()
        for later in range(1, ny):

            @pl.when(y < later)
            def _(later=later):
                carry_copy(y, later).wait_send()

    for step in order:
        rs_copy(step).wait_send()


def shards(
    q_in, k_in, v_in, conv_q, conv_k, conv_v, a_in, b_in, a_log, dt_bias, norm_weight, z_in, out_weight
):
    rows = q_in.shape[0]
    nz = v_in.shape[1] // DV
    nx = lax.axis_size("heads")
    ny = lax.axis_size("ctx") // (2 * nz)
    key_heads = nz // 2
    width = out_weight.shape[1] // nx
    hbm = pl.BlockSpec(memory_space=pltpu.HBM)
    vmem = pl.BlockSpec(memory_space=pltpu.VMEM)
    dma = pltpu.SemaphoreType.DMA
    message = (DK + TAIL, DK + DV)
    scratch = [
        pltpu.VMEM(q_in.shape, BF16),
        pltpu.VMEM(k_in.shape, BF16),
        pltpu.VMEM(v_in.shape, BF16),
        pltpu.VMEM(z_in.shape, BF16),
        pltpu.VMEM(out_weight.shape, BF16),
        pltpu.VMEM((nz, rows), F32),
        pltpu.VMEM((nz, rows), F32),
        pltpu.VMEM((1, nz), F32),
        pltpu.VMEM((1, nz), F32),
        pltpu.VMEM((1, DV), F32),
        pltpu.VMEM(conv_q.shape, BF16),
        pltpu.VMEM(conv_k.shape, BF16),
        pltpu.VMEM(conv_v.shape, BF16),
        pltpu.VMEM((TAIL, q_in.shape[1]), BF16),
        pltpu.VMEM((TAIL, k_in.shape[1]), BF16),
        pltpu.VMEM((TAIL, v_in.shape[1]), BF16),
        pltpu.VMEM((rows + 8, 2 * DV), F32),
        pltpu.VMEM((key_heads, rows, 2 * DV), BF16),
        pltpu.VMEM((key_heads, rows, DK), BF16),
        pltpu.VMEM((key_heads, rows, DK), BF16),
        pltpu.VMEM((2, nz) + message, BF16),
        pltpu.VMEM((nz // 2,) + message, BF16),
        pltpu.VMEM((nz,) + message, BF16),
        pltpu.VMEM((ny,) + message, BF16),
        pltpu.VMEM((nz, DK, DV), F32),
        pltpu.VMEM((nz, DK, DK), BF16),
        pltpu.VMEM((nz, 8, 128), F32),
        pltpu.VMEM((DK, DV), F32),
        pltpu.VMEM((nz, DK, DV), BF16),
        pltpu.VMEM((nz, DK, DV), BF16),
        pltpu.VMEM((nz, rows, 2 * DK), BF16),
        pltpu.VMEM((nz, rows, DV), F32),
        pltpu.VMEM((rows, nz * DV), BF16),
        pltpu.VMEM((nx - 1, rows, width), BF16),
        pltpu.VMEM((nx - 1, rows, width), BF16),
        dma((13,)),
        dma((3,)),
        dma((3,)),
        dma((nz,)),
        dma((nz,)),
        dma((nz // 2,)),
        dma((nz,)),
        dma((ny,)),
        dma((ny,)),
        dma((nz,)),
        dma((nz,)),
        dma((nz,)),
        dma((nz,)),
        dma((nx - 1,)),
        dma((nx - 1,)),
    ]
    call = pl.pallas_call(
        functools.partial(kernel, nx, ny, nz),
        out_shape=jax.ShapeDtypeStruct((rows, width), F32),
        in_specs=[hbm] * 13,
        out_specs=vmem,
        scratch_shapes=scratch,
        compiler_params=pltpu.CompilerParams(
            collective_id=0, has_side_effects=True, vmem_limit_bytes=60 * 1024 * 1024
        ),
        cost_estimate=pl.CostEstimate(
            flops=2_000_000_000, bytes_accessed=6_000_000, transcendentals=1_000_000
        ),
    )
    return call(
        q_in,
        k_in,
        v_in,
        z_in,
        out_weight,
        a_in.T,
        b_in.T,
        a_log.reshape(1, nz),
        dt_bias.reshape(1, nz),
        norm_weight.reshape(1, DV),
        conv_q,
        conv_k,
        conv_v,
    )


def solution(mesh):
    in_specs = (
        P("ctx", "heads"),
        P("ctx", "heads"),
        P("ctx", "heads"),
        P(None, "heads"),
        P(None, "heads"),
        P(None, "heads"),
        P("ctx", "heads"),
        P("ctx", "heads"),
        P("heads"),
        P("heads"),
        P(),
        P("ctx", "heads"),
        P("heads", None),
    )
    out_specs = P("ctx", "heads")
    return jax.shard_map(shards, mesh=mesh, in_specs=in_specs, out_specs=out_specs, check_vma=False)
```

time: 68.6 us -> 49.9 us (0.73)
  local copies, waits for them, and re-layouts: 12.2 us -> 1.67 us
  Pallas kernels: 55.9 us -> 48.1 us
    unnamed x25 -> x1, local copies, waits for them, and re-layouts: 12.2 us -> 1.67 us
    pallas_call x1, Pallas kernels: 55.9 us -> 48.1 us  [shards(): call(q_in, k_in, v_in, z_in, out_weight, a_in.T, b_in.T, a_log.reshape(1,...]
where the time goes in v2:
time: 49.9 us; the launch traced here: 49.8 us
  Pallas kernels  48.1 us (96%)
  local copies, waits for them, and re-layouts  1.67 us (3%)
    pallas_call x1, Pallas kernels, shards(): call(q_in, k_in, v_in, z_in, out_weight, a_in.T, b_in.T, a_log.reshape(1,...  48.1 us
    unnamed x1, local copies, waits for them, and re-layouts  1.67 us

profile of v2, /device:TPU:25, one launch (start us, length us, event | category | flops | bytes accessed | tf_op | source)
XLA Modules:
  0.0 49.8 jit_solution(3179330042740908193)
XLA Ops:
  0.0 48.1 %shard_map.127 = f32[128,512]{1,0:T(8,128)} custom-call(bf16[128,512]{1,0:T(8,128)(2,1)} %q_hbm.1, bf16[128,512]{1,0:T(8,128)(2,1)} %k_hbm.1, bf16[128,1024]{1,0:T(8,128)(2,1)} %v_hbm.1, bf16[128,1024]{1,0:T(8,128)(2,1)} %z_hbm.1, bf16[1024,2048]{1,0:T(8,128)(2,1)} %w_hbm.1, f32[8,128]{1,0:T(8,128)} %bitcast.5, f32[8,128]{1,0:T(8,128)} %bitcast.6, ...), custom_call_target="tpu_custom_call" | custom-call | flops 2000000000 | bytes 6000000 | tf_op jit(solution)/shard_map/pallas_call | solution.py:720
  48.1 1.7 %copy.15 = f32[128,512]{1,0:T(8,128)} copy(f32[128,512]{1,0:T(8,128)} %shard_map.127) | data formatting | bytes 524288

commit v3 on v2

v3 whole, which is shorter than its diff:
```python
import functools

import jax
import jax.numpy as jnp
from jax import lax
from jax.experimental import pallas as pl
from jax.experimental.pallas import tpu as pltpu
from jax.sharding import PartitionSpec as P

DK = 128
DV = 128
TAIL = 16
MESH = pl.DeviceIdType.MESH
F32 = jnp.float32
BF16 = jnp.bfloat16
HIGHEST = lax.Precision.HIGHEST


def split(value):
    high = value.astype(BF16)
    return high, (value - high.astype(F32)).astype(BF16)


def mm(left, right):
    return jnp.dot(left, right, preferred_element_type=F32)


def one_pass(left, right):
    return mm(left.astype(BF16), right.astype(BF16))


def split_left(left, right):
    high, low = split(left)
    return mm(jnp.concatenate([high, low], axis=1), jnp.concatenate([right, right], axis=0))


def split_right(left, right):
    high, low = split(right)
    return mm(jnp.concatenate([left, left], axis=1), jnp.concatenate([high, low], axis=0))


def split_both(left, right):
    left_high, left_low = split(left)
    right_high, right_low = split(right)
    return mm(
        jnp.concatenate([left_high, left_low], axis=1),
        jnp.concatenate([right_high, right_high], axis=0),
    ) + mm(left_high, right_low)


def silu(value):
    return value * (1.0 / (1.0 + jnp.exp(-value)))


def three_parts(value):
    first = value.astype(BF16).astype(F32)
    second = (value - first).astype(BF16).astype(F32)
    return first, second, value - first - second


def pack_decay(decay, width):
    row = lax.broadcasted_iota(jnp.int32, (TAIL, width), 0)
    first, second, third = three_parts(decay)
    zero = jnp.zeros((TAIL, width), F32)
    block = jnp.where(row == 0, first, jnp.where(row == 1, second, jnp.where(row == 2, third, zero)))
    return block.astype(BF16)


def kernel(
    nx,
    ny,
    nz,
    q_hbm,
    k_hbm,
    v_hbm,
    z_hbm,
    w_hbm,
    a_hbm,
    b_hbm,
    alog_hbm,
    bias_hbm,
    gain_hbm,
    cq_hbm,
    ck_hbm,
    cv_hbm,
    out_ref,
    q_in,
    k_in,
    v_in,
    z_in,
    w_in,
    a_in,
    b_in,
    alog_ref,
    bias_ref,
    gain_ref,
    cq_ref,
    ck_ref,
    cv_ref,
    halo_q,
    halo_k,
    halo_v,
    ext,
    qc_all,
    kc_all,
    vc_all,
    up_out,
    up_in,
    carry,
    pre_state,
    pre_map,
    pre_decay,
    sigma,
    down_out,
    down_in,
    reads,
    local,
    normed,
    pass_out,
    rs_out,
    rs_in,
    load_sem,
    swap_send,
    swap_recv,
    halo_send,
    halo_recv,
    up_send,
    up_recv,
    y_send,
    y_recv,
    down_send,
    down_recv,
    pass_sem,
    rs_send,
    rs_recv,
):
    rows = out_ref.shape[0]
    width = out_ref.shape[1]
    set_heads = nz // 2
    set_keys = nz // 4
    ring = 2 * nz
    count = ny * ring
    me = lax.axis_index("ctx")
    x = lax.axis_index("heads")
    y = me // ring
    place = lax.rem(me, ring)
    z = place // 2
    core = lax.rem(place, 2)
    chip = me // 2
    chips = count // 2
    partner = me + 1 - 2 * core
    heads = range(set_heads)
    keys = range(set_keys)
    both_shards = range(2)
    units = [(u, h) for u in both_shards for h in heads]
    key_units = [(u, s) for u in both_shards for s in keys]

    sender_core = z // set_heads
    owns = core != sender_core

    def owner_of(h):
        return y * ring + 2 * (set_heads * core + h) + 1 - core

    def cols_of(which, size):
        return pl.ds(pl.multiple_of(which * size, 128), size)

    streams = (
        (k_hbm, k_in, halo_k, ck_ref, kc_all, set_keys * DK),
        (v_hbm, v_in, halo_v, cv_ref, vc_all, set_heads * DV),
        (q_hbm, q_in, halo_q, cq_ref, qc_all, set_keys * DK),
    )
    wide = [(source, target, size) for source, target, _, _, _, size in streams]
    wide.append((z_hbm, z_in, set_heads * DV))
    pairs = [(source.at[:, cols_of(core, size)], target.at[core]) for source, target, size in wide]
    pairs += [
        (a_hbm, a_in.at[core]),
        (b_hbm, b_in.at[core]),
        (alog_hbm, alog_ref),
        (bias_hbm, bias_ref),
        (ck_hbm, ck_ref),
        (cv_hbm, cv_ref),
        (cq_hbm, cq_ref),
        (gain_hbm, gain_ref),
        (w_hbm, w_in),
    ]
    loads = [
        pltpu.make_async_copy(source, target, load_sem.at[i])
        for i, (source, target) in enumerate(pairs)
    ]
    first = [0, 1, 2, 8, 9, 10, 4, 5, 6, 7]
    rest = [3, 11, 12]
    for i in first + rest:
        loads[i].start()

    barrier = pltpu.get_barrier_semaphore()

    def greet(ctx, heads):
        pl.semaphore_signal(barrier, inc=1, device_id=(ctx, heads), device_id_type=MESH)

    for step in range(1, ring):
        greet(y * ring + lax.rem(place + step, ring), x)
    for step in range(1, ny):
        greet(lax.rem(me + step * ring, count), x)
    for step in range(1, nx):
        greet(me, lax.rem(x + step, nx))
    over = jnp.logical_and(place == ring - 1, me < count - 1)
    under = jnp.logical_and(z == 0, y > 0)

    @pl.when(over)
    def _():
        greet(me + 1, x)
        greet(me + 2, x)

    @pl.when(under)
    def _():
        greet(y * ring - 1, x)

    pl.semaphore_wait(
        barrier,
        (ring - 1) + (ny - 1) + (nx - 1) + 2 * over.astype(jnp.int32) + under.astype(jnp.int32),
    )

    def halo_copies(side):
        return [
            pltpu.make_async_remote_copy(
                src_ref=source.at[pl.ds(rows - TAIL, TAIL), cols_of(side, size)],
                dst_ref=target,
                send_sem=halo_send.at[3 * side + i],
                recv_sem=halo_recv.at[i],
                device_id=(2 * lax.rem(chip + 1, chips) + side, x),
                device_id_type=MESH,
            )
            for i, (source, _, target, _, _, size) in enumerate(streams)
        ]

    sends_halo = jnp.logical_and(core == 1, chip < chips - 1)

    @pl.when(sends_halo)
    def _():
        for side in range(2):
            for copy in halo_copies(side):
                copy.start()

    def swap_copies(shard):
        return [
            pltpu.make_async_remote_copy(
                src_ref=source,
                dst_ref=target.at[shard],
                send_sem=swap_send.at[i],
                recv_sem=swap_recv.at[i],
                device_id=(partner, x),
                device_id_type=MESH,
            )
            for i, (source, target) in enumerate(
                [
                    (source.at[:, cols_of(1 - core, size)], target)
                    for source, target, size in wide[:3]
                ]
                + [(a_hbm, a_in), (b_hbm, b_in)]
                + [
                    (source.at[:, cols_of(1 - core, size)], target)
                    for source, target, size in wide[3:]
                ]
            )
        ]

    swap = swap_copies(core)
    swapped = swap_copies(1 - core)
    for copy in swap:
        copy.start()

    @pl.when(chip == 0)
    def _():
        halo_k[...] = jnp.zeros_like(halo_k)
        halo_v[...] = jnp.zeros_like(halo_v)
        halo_q[...] = jnp.zeros_like(halo_q)

    def conv(before, data, taps_ref, size):
        height = data.shape[0]
        ext[0:8, 0:size] = before
        ext[8 : 8 + height, 0:size] = data.astype(F32)
        taps = taps_ref[:, cols_of(core, size)].astype(F32)
        total = jnp.zeros((height, size), F32)
        for j in range(4):
            total = total + taps[j : j + 1] * ext[5 + j : 5 + j + height, 0:size]
        return silu(total).astype(BF16)

    for i in first:
        loads[i].wait()
    for _, data, _, taps_ref, result, size in streams:
        result[core] = conv(jnp.zeros((8, size), F32), data[core], taps_ref, size)

    row = lax.broadcasted_iota(jnp.int32, (rows, rows), 0)
    col = lax.broadcasted_iota(jnp.int32, (rows, rows), 1)
    upto = row >= col
    strict = row > col
    apart = jnp.bitwise_xor(row, col)

    for i in range(3):
        swapped[i].wait_recv()
    for _, data, _, taps_ref, result, size in streams:
        result[1 - core] = conv(jnp.zeros((8, size), F32), data[1 - core], taps_ref, size)

    for i in range(3, 5):
        swapped[i].wait_recv()
    head_row = lax.broadcasted_iota(jnp.int32, (nz, nz), 0)
    head_lane = lax.broadcasted_iota(jnp.int32, (nz, nz), 1)

    def per_head(values):
        return jnp.sum(jnp.where(head_row == head_lane, values, 0.0), axis=1, keepdims=True)

    slot = lax.broadcasted_iota(jnp.int32, (128, nz), 0)
    from_head = lax.broadcasted_iota(jnp.int32, (128, nz), 1)

    def placing(start):
        wanted = set_heads * core + slot - start
        inside = jnp.logical_and(slot >= start, slot < start + set_heads)
        return jnp.where(jnp.logical_and(inside, wanted == from_head), 1.0, 0.0)

    def exact(left, right):
        return jnp.dot(left, right, preferred_element_type=F32, precision=HIGHEST)

    bias, rate = per_head(bias_ref[...]), jnp.exp(per_head(alog_ref[...]))
    before_or_at = jnp.where(row <= col, 1.0, 0.0)
    by_row = jnp.zeros((128, rows), F32)
    for u in both_shards:
        gate_in = a_in[u] + bias
        softplus = jnp.maximum(gate_in, 0.0) + jnp.log1p(jnp.exp(-jnp.abs(gate_in)))
        cumulative = exact(-rate * softplus, before_or_at)
        beta = 1.0 / (1.0 + jnp.exp(-b_in[u]))
        by_row = by_row + exact(placing(16 * u), cumulative)
        by_row = by_row + exact(placing(16 * u + set_heads), beta)
    columns = jnp.transpose(by_row)

    @pl.when(chip > 0)
    def _():
        for copy in halo_copies(0):
            copy.wait_recv()

    def inverse_norm(block):
        entries = block.astype(F32)
        return lax.rsqrt(jnp.sum(entries * entries, axis=1, keepdims=True) + 1e-6)

    for _, data, halo, taps_ref, result, size in streams:
        for u in both_shards:
            before = halo[...] if u == 0 else data[0, rows - TAIL : rows, :]
            result[u, 0:TAIL, :] = conv(
                before.astype(F32)[8:16], data[u, 0:TAIL, :], taps_ref, size
            )

    def key_of(u, s):
        return kc_all[u, :, s * DK : (s + 1) * DK]

    def query_of(u, s):
        return qc_all[u, :, s * DK : (s + 1) * DK]

    wide_lane = lax.broadcasted_iota(jnp.int32, (rows, 128), 1)
    for u, s in key_units:
        place_of = 16 * u + 2 * set_heads + s
        columns = jnp.where(wide_lane == place_of, inverse_norm(key_of(u, s)), columns)
        columns = jnp.where(
            wide_lane == place_of + set_keys, inverse_norm(query_of(u, s)) * DK**-0.5, columns
        )
    by_row = jnp.transpose(columns)

    def column(u, index):
        return columns[:, 16 * u + index : 16 * u + index + 1]

    def lane_row(u, index):
        return by_row[16 * u + index : 16 * u + index + 1, :]

    gram, query_gram, key_t = {}, {}, {}
    for u, s in key_units:
        contract = (((1,), (1,)), ((), ()))
        gram[u, s] = lax.dot_general(
            key_of(u, s), key_of(u, s), contract, preferred_element_type=F32
        )
        query_gram[u, s] = lax.dot_general(
            query_of(u, s), key_of(u, s), contract, preferred_element_type=F32
        )
        key_t[u, s] = jnp.transpose(key_of(u, s).astype(F32)).astype(BF16)
    within, lower, inverse = {}, {}, {}
    for u, h in units:
        s = h // 2
        gaps = column(u, h) - lane_row(u, h)
        within[u, h] = jnp.exp(jnp.where(upto, gaps, -1e30)) * lane_row(u, 2 * set_heads + s)
        scale = column(u, set_heads + h) * column(u, 2 * set_heads + s)
        lower[u, h] = jnp.where(strict, scale * gram[u, s] * within[u, h], 0.0)
        inverse[u, h] = jnp.where(apart == 1, -lower[u, h], 0.0)
    level = 1
    while (1 << level) < rows:
        inner = {}
        for i in units:
            block = jnp.where((apart >> level) == 1, lower[i], 0.0)
            inner[i] = block + one_pass(block, inverse[i])
        for i in units:
            inverse[i] = inverse[i] - inner[i] - one_pass(inverse[i], inner[i])
        level += 1
    values, maps, shard_maps, decays = {}, {}, {}, {}
    for u, h in units:
        s = h // 2
        solve = jnp.where(row == col, 1.0, inverse[u, h]) * lane_row(u, set_heads + h)
        values[u, h] = split_left(solve, vc_all[u, :, h * DV : (h + 1) * DV])
        key_solve = solve * (jnp.exp(lane_row(u, h)) * lane_row(u, 2 * set_heads + s))
        maps[u, h] = split_left(key_solve, key_of(u, s))
    for u, h in units:
        s = h // 2
        last = column(u, h)[rows - 1 : rows, :]
        tail = jnp.exp(last - column(u, h)) * column(u, 2 * set_heads + s)
        both = jnp.concatenate([values[u, h] * tail, maps[u, h] * tail], axis=1)
        shard_maps[u, h] = split_right(key_t[u, s], both)
        decays[u, h] = jnp.exp(last)

    eye = row[0:DK, 0:DK] == col[0:DK, 0:DK]

    def decay_of(block):
        return jnp.sum(block.astype(F32), axis=0, keepdims=True)

    def map_of(message, decay):
        return jnp.where(eye, decay[:, 0:1], 0.0) - message[:, DV:].astype(F32)

    def compose(message, decay, carried):
        state = decay * carried[:, 0:DV] + message[:, 0:DV].astype(F32)
        fresh = jnp.concatenate([state, decay * carried[:, DV:]], axis=1)
        return fresh - mm(message[:, DV:].astype(BF16), carried.astype(BF16))

    def put_message(target, carried, decay):
        target[0:DK, 0:DV] = carried[:, 0:DV].astype(BF16)
        target[0:DK, DV:] = map_of(carried, decay).astype(BF16)
        target[DK:, :] = pack_decay(decay, DK + DV)

    def up_copy(h):
        return pltpu.make_async_remote_copy(
            src_ref=up_out.at[h],
            dst_ref=up_in.at[z],
            send_sem=up_send.at[h],
            recv_sem=up_recv.at[z],
            device_id=(owner_of(h), x),
            device_id_type=MESH,
        )

    joined = {}
    for h in heads:
        early = shard_maps[0, h]
        carried = jnp.concatenate([early[:, 0:DV], map_of(early, decays[0, h])], axis=1)
        joined[h] = compose(shard_maps[1, h], decays[1, h], carried)
    for h in heads:
        put_message(up_out.at[h], joined[h], decays[0, h] * decays[1, h])
        up_copy(h).start()

    for u, h in units:
        s = h // 2
        scale = column(u, 2 * set_heads + set_keys + s)
        attend = jnp.where(upto, query_gram[u, s] * within[u, h] * scale, 0.0)
        both = split_both(attend, jnp.concatenate([values[u, h], maps[u, h]], axis=1))
        fixed = both[:, 0:DV]
        read = jnp.exp(column(u, h)) * scale * query_of(u, s).astype(F32) - both[:, DV:]
        if u == 1:
            moved = split_both(read, shard_maps[0, h])
            fixed = fixed + moved[:, 0:DV]
            read = decays[0, h] * read - moved[:, DV:]
        high, low = split(read)
        local[h, u * rows : (u + 1) * rows, :] = fixed
        reads[h, u * rows : (u + 1) * rows, 0:DK] = high
        reads[h, u * rows : (u + 1) * rows, DK:] = low

    def carry_copy(source, target_y):
        return pltpu.make_async_remote_copy(
            src_ref=carry.at[source],
            dst_ref=carry.at[source],
            send_sem=y_send.at[target_y],
            recv_sem=y_recv.at[source],
            device_id=(target_y * ring + place, x),
            device_id_type=MESH,
        )

    def down_copy(target):
        slot = lax.rem(z, set_heads)
        return pltpu.make_async_remote_copy(
            src_ref=down_out.at[target],
            dst_ref=down_in.at[slot],
            send_sem=down_send.at[target],
            recv_sem=down_recv.at[slot],
            device_id=(y * ring + 2 * target + sender_core, x),
            device_id_type=MESH,
        )

    @pl.when(owns)
    def _():
        pre_state[0] = jnp.zeros((DK, DV), F32)
        pre_map[0] = jnp.zeros((DK, DK), BF16)
        pre_decay[0] = jnp.ones((8, 128), F32)
        total_decay = None
        carried = None
        for j in range(nz):
            pltpu.make_async_remote_copy(
                src_ref=up_out.at[0],
                dst_ref=up_in.at[j],
                send_sem=up_send.at[0],
                recv_sem=up_recv.at[j],
                device_id=(partner, x),
                device_id_type=MESH,
            ).wait_recv()
            message = up_in[j, 0:DK, :]
            decay = decay_of(up_in[j, DK:, 0:DK])
            if j == 0:
                total_decay = decay
                carried = jnp.concatenate(
                    [message[:, 0:DV].astype(F32), map_of(message, decay)], axis=1
                )
            else:
                carried = compose(message, decay, carried)
                total_decay = total_decay * decay
            if j < nz - 1:
                pre_state[j + 1] = carried[:, 0:DV]
                pre_map[j + 1] = map_of(carried, total_decay).astype(BF16)
                pre_decay[j + 1] = jnp.broadcast_to(total_decay, (8, 128))
        put_message(carry.at[y], carried, total_decay[:, 0:1])

        for later in range(1, ny):

            @pl.when(y < later)
            def _(later=later):
                carry_copy(y, later).start()

        sigma[...] = jnp.zeros((DK, DV), F32)
        for earlier in range(ny - 1):

            @pl.when(y > earlier)
            def _(earlier=earlier):
                carry_copy(earlier, y).wait_recv()
                message = carry[earlier]
                state = sigma[...]
                sigma[...] = (
                    decay_of(message[DK:, 0:DV]) * state
                    - mm(message[0:DK, DV:], state.astype(BF16))
                    + message[0:DK, 0:DV].astype(F32)
                )

        start_state = sigma[...]
        rounded = start_state.astype(BF16)
        for offset in sorted(range(nz), key=lambda offset: -min(offset, nz - offset)):
            target = lax.rem(z + offset, nz)
            down_out[target] = (
                pre_decay[target, 0:1, :] * start_state
                - mm(pre_map[target], rounded)
                + pre_state[target]
            ).astype(BF16)
            down_copy(target).start()

    for i in rest:
        loads[i].wait()
    swapped[5].wait_recv()

    cores = {}
    for h in heads:
        pltpu.make_async_remote_copy(
            src_ref=down_out.at[0],
            dst_ref=down_in.at[h],
            send_sem=down_send.at[0],
            recv_sem=down_recv.at[h],
            device_id=(owner_of(h), x),
            device_id_type=MESH,
        ).wait_recv()
    for h in heads:
        state = down_in[h]
        cores[h] = mm(reads[h], jnp.concatenate([state, state], axis=0)) + local[h]
    hand_over = pltpu.make_async_remote_copy(
        src_ref=pass_out.at[1 - core],
        dst_ref=normed.at[core],
        send_sem=pass_sem.at[0],
        recv_sem=pass_sem.at[1],
        device_id=(partner, x),
        device_id_type=MESH,
    )
    for h in heads:
        power = jnp.mean(cores[h] * cores[h], axis=1, keepdims=True)
        gated = cores[h] * lax.rsqrt(power + 1e-6) * gain_ref[...]
        cols = slice(h * DV, (h + 1) * DV)
        for u in both_shards:
            gate = silu(z_in[u, :, cols].astype(F32))
            pass_out[u, :, cols] = (gated[u * rows : (u + 1) * rows] * gate).astype(BF16)
    hand_over.start()
    normed[core] = pass_out[core]
    pltpu.make_async_remote_copy(
        src_ref=pass_out.at[core],
        dst_ref=normed.at[1 - core],
        send_sem=pass_sem.at[0],
        recv_sem=pass_sem.at[1],
        device_id=(partner, x),
        device_id_type=MESH,
    ).wait_recv()

    depth = set_heads * DV

    def part(step):
        cols = cols_of(lax.rem(x + step, nx), width)
        return mm(normed[0], w_in[0:depth, cols]) + mm(normed[1], w_in[depth:, cols])

    def rs_copy(step):
        return pltpu.make_async_remote_copy(
            src_ref=rs_out.at[step - 1],
            dst_ref=rs_in.at[step - 1],
            send_sem=rs_send.at[step - 1],
            recv_sem=rs_recv.at[step - 1],
            device_id=(me, lax.rem(x + step, nx)),
            device_id_type=MESH,
        )

    order = sorted(range(1, nx), key=lambda step: -min(step, nx - step))
    for step in order:
        rs_out[step - 1] = part(step).astype(BF16)
        rs_copy(step).start()
    total = part(0)
    for step in reversed(order):
        rs_copy(step).wait_recv()
        total = total + rs_in[step - 1].astype(F32)
    out_ref[...] = total

    @pl.when(sends_halo)
    def _():
        for side in range(2):
            for copy in halo_copies(side):
                copy.wait_send()

    for copy in swap:
        copy.wait_send()
    for h in heads:
        up_copy(h).wait_send()

    @pl.when(owns)
    def _():
        for target in range(nz):
            down_copy(target).wait_send()
        for later in range(1, ny):

            @pl.when(y < later)
            def _(later=later):
                carry_copy(y, later).wait_send()

    hand_over.wait_send()
    for step in order:
        rs_copy(step).wait_send()


def shards(
    q_in, k_in, v_in, conv_q, conv_k, conv_v, a_in, b_in, a_log, dt_bias, norm_weight, z_in, out_weight
):
    rows = q_in.shape[0]
    nz = v_in.shape[1] // DV
    nx = lax.axis_size("heads")
    ny = lax.axis_size("ctx") // (2 * nz)
    width = out_weight.shape[1] // nx
    half = q_in.shape[1] // 2
    half_v = v_in.shape[1] // 2
    hbm = pl.BlockSpec(memory_space=pltpu.HBM)
    vmem = pl.BlockSpec(memory_space=pltpu.VMEM)
    dma = pltpu.SemaphoreType.DMA
    message = (DK + TAIL, DK + DV)
    scratch = [
        pltpu.VMEM((2, rows, half), BF16),
        pltpu.VMEM((2, rows, half), BF16),
        pltpu.VMEM((2, rows, half_v), BF16),
        pltpu.VMEM((2, rows, half_v), BF16),
        pltpu.VMEM(out_weight.shape, BF16),
        pltpu.VMEM((2, nz, rows), F32),
        pltpu.VMEM((2, nz, rows), F32),
        pltpu.VMEM((1, nz), F32),
        pltpu.VMEM((1, nz), F32),
        pltpu.VMEM((1, DV), F32),
        pltpu.VMEM(conv_q.shape, BF16),
        pltpu.VMEM(conv_k.shape, BF16),
        pltpu.VMEM(conv_v.shape, BF16),
        pltpu.VMEM((TAIL, half), BF16),
        pltpu.VMEM((TAIL, half), BF16),
        pltpu.VMEM((TAIL, half_v), BF16),
        pltpu.VMEM((rows + 8, half_v), F32),
        pltpu.VMEM((2, rows, half), BF16),
        pltpu.VMEM((2, rows, half), BF16),
        pltpu.VMEM((2, rows, half_v), BF16),
        pltpu.VMEM((nz // 2,) + message, BF16),
        pltpu.VMEM((nz,) + message, BF16),
        pltpu.VMEM((ny,) + message, BF16),
        pltpu.VMEM((nz, DK, DV), F32),
        pltpu.VMEM((nz, DK, DK), BF16),
        pltpu.VMEM((nz, 8, 128), F32),
        pltpu.VMEM((DK, DV), F32),
        pltpu.VMEM((nz, DK, DV), BF16),
        pltpu.VMEM((nz // 2, DK, DV), BF16),
        pltpu.VMEM((nz // 2, 2 * rows, 2 * DK), BF16),
        pltpu.VMEM((nz // 2, 2 * rows, DV), F32),
        pltpu.VMEM((2, rows, half_v), BF16),
        pltpu.VMEM((2, rows, half_v), BF16),
        pltpu.VMEM((nx - 1, rows, width), BF16),
        pltpu.VMEM((nx - 1, rows, width), BF16),
        dma((13,)),
        dma((6,)),
        dma((6,)),
        dma((6,)),
        dma((3,)),
        dma((nz // 2,)),
        dma((nz,)),
        dma((ny,)),
        dma((ny,)),
        dma((nz,)),
        dma((nz // 2,)),
        dma((2,)),
        dma((nx - 1,)),
        dma((nx - 1,)),
    ]
    call = pl.pallas_call(
        functools.partial(kernel, nx, ny, nz),
        out_shape=jax.ShapeDtypeStruct((rows, width), F32),
        in_specs=[hbm] * 13,
        out_specs=vmem,
        scratch_shapes=scratch,
        compiler_params=pltpu.CompilerParams(
            collective_id=0, has_side_effects=True, vmem_limit_bytes=40 * 1024 * 1024
        ),
        cost_estimate=pl.CostEstimate(
            flops=2_000_000_000, bytes_accessed=6_000_000, transcendentals=1_000_000
        ),
    )
    operands = (
        q_in,
        k_in,
        v_in,
        z_in,
        out_weight,
        a_in.T,
        b_in.T,
        a_log.reshape(1, nz),
        dt_bias.reshape(1, nz),
        norm_weight.reshape(1, DV),
        conv_q,
        conv_k,
        conv_v,
    )
    return call(*(pltpu.with_memory_space_constraint(value, pltpu.HBM) for value in operands))


def solution(mesh):
    in_specs = (
        P("ctx", "heads"),
        P("ctx", "heads"),
        P("ctx", "heads"),
        P(None, "heads"),
        P(None, "heads"),
        P(None, "heads"),
        P("ctx", "heads"),
        P("ctx", "heads"),
        P("heads"),
        P("heads"),
        P(),
        P("ctx", "heads"),
        P("heads", None),
    )
    out_specs = P("ctx", "heads")
    return jax.shard_map(shards, mesh=mesh, in_specs=in_specs, out_specs=out_specs, check_vma=False)
```

time: 49.9 us -> 45.9 us (0.920)
  Pallas kernels: 48.1 us -> 45.1 us
  local copies, waits for them, and re-layouts: 1.67 us -> 0.71 us
    pallas_call x1, Pallas kernels: 48.1 us -> 45.1 us  [shards(): call(*(pltpu.with_memory_space_constraint(value, pltpu.HBM) for value in...]
    unnamed x1, local copies, waits for them, and re-layouts: 1.67 us -> 0.71 us
where the time goes in v3:
time: 45.9 us; the launch traced here: 45.8 us
  Pallas kernels  45.1 us (98%)
  local copies, waits for them, and re-layouts  0.71 us (2%)
    pallas_call x1, Pallas kernels, shards(): call(*(pltpu.with_memory_space_constraint(value, pltpu.HBM) for value in...  45.1 us

profile of v3, /device:TPU:25, one launch (start us, length us, event | category | flops | bytes accessed | tf_op | source)
XLA Modules:
  0.0 45.8 jit_solution(2595625800129977997)
XLA Ops:
  0.0 45.1 %shard_map.127 = f32[128,512]{1,0:T(8,128)S(1)} custom-call(bf16[128,512]{1,0:T(8,128)(2,1)} %q_hbm.1, bf16[128,512]{1,0:T(8,128)(2,1)} %k_hbm.1, bf16[128,1024]{1,0:T(8,128)(2,1)} %v_hbm.1, bf16[128,1024]{1,0:T(8,128)(2,1)} %z_hbm.1, bf16[1024,2048]{1,0:T(8,128)(2,1)} %w_hbm.1, f32[8,128]{1,0:T(8,128)} %bitcast.5, f32[8,128]{1,0:T(8,128)} %bitcast.6, ...), custom_call_target="tpu_custom_call" | custom-call | flops 2000000000 | bytes 6000000 | tf_op jit(solution)/shard_map/pallas_call | solution.py:739
  45.1 0.7 %copy.15 = f32[128,512]{1,0:T(8,128)} copy(f32[128,512]{1,0:T(8,128)S(1)} %shard_map.127) | data formatting | bytes 524288

commit v4 on v3

--- a/solution.py
+++ b/solution.py
@@ -104,6 +104,8 @@
     qc_all,
     kc_all,
     vc_all,
+    decay_out,
+    decay_in,
     up_out,
     up_in,
     carry,
@@ -117,6 +119,7 @@
     local,
     normed,
     pass_out,
+    gates,
     rs_out,
     rs_in,
     load_sem,
@@ -124,6 +127,8 @@
     swap_recv,
     halo_send,
     halo_recv,
+    decay_send,
+    decay_recv,
     up_send,
     up_recv,
     y_send,
@@ -331,6 +336,23 @@
         by_row = by_row + exact(placing(16 * u), cumulative)
         by_row = by_row + exact(placing(16 * u + set_heads), beta)
     columns = jnp.transpose(by_row)
+
+    def decay_copy(h):
+        return pltpu.make_async_remote_copy(
+            src_ref=decay_out.at[h],
+            dst_ref=decay_in.at[z],
+            send_sem=decay_send.at[h],
+            recv_sem=decay_recv.at[z],
+            device_id=(owner_of(h), x),
+            device_id_type=MESH,
+        )
+
+    for h in heads:
+        chip_decay = [
+            jnp.exp(columns[rows - 1 : rows, 16 * u + h : 16 * u + h + 1]) for u in both_shards
+        ]
+        decay_out[h] = jnp.broadcast_to(chip_decay[0] * chip_decay[1], (8, 128))
+        decay_copy(h).start()
 
     @pl.when(chip > 0)
     def _():
@@ -424,10 +446,9 @@
         fresh = jnp.concatenate([state, decay * carried[:, DV:]], axis=1)
         return fresh - mm(message[:, DV:].astype(BF16), carried.astype(BF16))
 
-    def put_message(target, carried, decay):
+    def put_maps(target, carried, decay):
         target[0:DK, 0:DV] = carried[:, 0:DV].astype(BF16)
         target[0:DK, DV:] = map_of(carried, decay).astype(BF16)
-        target[DK:, :] = pack_decay(decay, DK + DV)
 
     def up_copy(h):
         return pltpu.make_async_remote_copy(
@@ -445,8 +466,14 @@
         carried = jnp.concatenate([early[:, 0:DV], map_of(early, decays[0, h])], axis=1)
         joined[h] = compose(shard_maps[1, h], decays[1, h], carried)
     for h in heads:
-        put_message(up_out.at[h], joined[h], decays[0, h] * decays[1, h])
-        up_copy(h).start()
+        put_maps(up_out.at[h], joined[h], decays[0, h] * decays[1, h])
+    far_first = sorted(range(nz), key=lambda offset: -min(offset, nz - offset))
+    for offset in far_first:
+        target_chip = lax.rem(z + offset, nz)
+
+        @pl.when(target_chip // set_heads == core)
+        def _(h=lax.rem(target_chip, set_heads)):
+            up_copy(h).start()
 
     for u, h in units:
         s = h // 2
@@ -485,43 +512,68 @@
             device_id_type=MESH,
         )
 
+    for i in rest:
+        loads[i].wait()
+    swapped[5].wait_recv()
+    for h in heads:
+        cols = slice(h * DV, (h + 1) * DV)
+        for u in both_shards:
+            gates[u, :, cols] = silu(z_in[u, :, cols].astype(F32)) * gain_ref[...]
+
     @pl.when(owns)
     def _():
         pre_state[0] = jnp.zeros((DK, DV), F32)
         pre_map[0] = jnp.zeros((DK, DK), BF16)
         pre_decay[0] = jnp.ones((8, 128), F32)
-        total_decay = None
-        carried = None
+        spans = {}
         for j in range(nz):
-            pltpu.make_async_remote_copy(
-                src_ref=up_out.at[0],
-                dst_ref=up_in.at[j],
-                send_sem=up_send.at[0],
-                recv_sem=up_recv.at[j],
-                device_id=(partner, x),
-                device_id_type=MESH,
-            ).wait_recv()
-            message = up_in[j, 0:DK, :]
-            decay = decay_of(up_in[j, DK:, 0:DK])
-            if j == 0:
-                total_decay = decay
-                carried = jnp.concatenate(
-                    [message[:, 0:DV].astype(F32), map_of(message, decay)], axis=1
-                )
-            else:
-                carried = compose(message, decay, carried)
-                total_decay = total_decay * decay
-            if j < nz - 1:
-                pre_state[j + 1] = carried[:, 0:DV]
-                pre_map[j + 1] = map_of(carried, total_decay).astype(BF16)
-                pre_decay[j + 1] = jnp.broadcast_to(total_decay, (8, 128))
-        put_message(carry.at[y], carried, total_decay[:, 0:1])
+            for source, target, sent, received in (
+                (decay_out, decay_in, decay_send, decay_recv),
+                (up_out, up_in, up_send, up_recv),
+            ):
+                pltpu.make_async_remote_copy(
+                    src_ref=source.at[0],
+                    dst_ref=target.at[j],
+                    send_sem=sent.at[0],
+                    recv_sem=received.at[j],
+                    device_id=(partner, x),
+                    device_id_type=MESH,
+                ).wait_recv()
+            decay = decay_in[j, 0:1, :]
+            state, taken = up_in[j, :, 0:DV].astype(F32), up_in[j, :, DV:].astype(F32)
+            carried = jnp.concatenate([state, jnp.where(eye, decay, 0.0) - taken], axis=1)
+            spans[j, j + 1] = (carried, decay)
+
+        def after(early, late):
+            (carried, decay), (later_maps, later_decay) = spans[early], spans[late]
+            message = jnp.concatenate(
+                [later_maps[:, 0:DV], map_of(later_maps, later_decay)], axis=1
+            )
+            spans[early[0], late[1]] = (compose(message, later_decay, carried), decay * later_decay)
+
+        size = 1
+        while size < nz:
+            for start in range(0, nz, 2 * size):
+                after((start, start + size), (start + size, start + 2 * size))
+            size *= 2
+        carried, total_decay = spans[0, nz]
+        put_maps(carry.at[y], carried, total_decay)
+        carry[y, DK:, :] = pack_decay(total_decay[:, 0:1], DK + DV)
 
         for later in range(1, ny):
 
             @pl.when(y < later)
             def _(later=later):
                 carry_copy(y, later).start()
+
+        for j in range(1, nz):
+            if (0, j) not in spans:
+                size = j & -j
+                after((0, j - size), (j - size, j))
+            carried, total_decay = spans[0, j]
+            pre_state[j] = carried[:, 0:DV]
+            pre_map[j] = map_of(carried, total_decay).astype(BF16)
+            pre_decay[j] = jnp.broadcast_to(total_decay, (8, 128))
 
         sigma[...] = jnp.zeros((DK, DV), F32)
         for earlier in range(ny - 1):
@@ -539,7 +591,7 @@
 
         start_state = sigma[...]
         rounded = start_state.astype(BF16)
-        for offset in sorted(range(nz), key=lambda offset: -min(offset, nz - offset)):
+        for offset in far_first:
             target = lax.rem(z + offset, nz)
             down_out[target] = (
                 pre_decay[target, 0:1, :] * start_state
@@ -547,10 +599,6 @@
                 + pre_state[target]
             ).astype(BF16)
             down_copy(target).start()
-
-    for i in rest:
-        loads[i].wait()
-    swapped[5].wait_recv()
 
     cores = {}
     for h in heads:
@@ -567,7 +615,7 @@
         cores[h] = mm(reads[h], jnp.concatenate([state, state], axis=0)) + local[h]
     hand_over = pltpu.make_async_remote_copy(
         src_ref=pass_out.at[1 - core],
-        dst_ref=normed.at[core],
+        dst_ref=normed,
         send_sem=pass_sem.at[0],
         recv_sem=pass_sem.at[1],
         device_id=(partner, x),
@@ -575,27 +623,29 @@
     )
     for h in heads:
         power = jnp.mean(cores[h] * cores[h], axis=1, keepdims=True)
-        gated = cores[h] * lax.rsqrt(power + 1e-6) * gain_ref[...]
+        scaled = cores[h] * lax.rsqrt(power + 1e-6)
         cols = slice(h * DV, (h + 1) * DV)
         for u in both_shards:
-            gate = silu(z_in[u, :, cols].astype(F32))
-            pass_out[u, :, cols] = (gated[u * rows : (u + 1) * rows] * gate).astype(BF16)
+            part_rows = scaled[u * rows : (u + 1) * rows]
+            pass_out[u, :, cols] = (part_rows * gates[u, :, cols]).astype(BF16)
     hand_over.start()
-    normed[core] = pass_out[core]
+
+    depth = set_heads * DV
+
+    def part(step, which, operand):
+        depth_rows = pl.ds(pl.multiple_of(which * depth, 128), depth)
+        return mm(operand, w_in[depth_rows, cols_of(lax.rem(x + step, nx), width)])
+
+    order = sorted(range(1, nx), key=lambda step: -min(step, nx - step))
+    parts = {step: part(step, core, pass_out[core]) for step in order}
     pltpu.make_async_remote_copy(
         src_ref=pass_out.at[core],
-        dst_ref=normed.at[1 - core],
+        dst_ref=normed,
         send_sem=pass_sem.at[0],
         recv_sem=pass_sem.at[1],
         device_id=(partner, x),
         device_id_type=MESH,
     ).wait_recv()
-
-    depth = set_heads * DV
-
-    def part(step):
-        cols = cols_of(lax.rem(x + step, nx), width)
-        return mm(normed[0], w_in[0:depth, cols]) + mm(normed[1], w_in[depth:, cols])
 
     def rs_copy(step):
         return pltpu.make_async_remote_copy(
@@ -607,11 +657,10 @@
             device_id_type=MESH,
         )
 
-    order = sorted(range(1, nx), key=lambda step: -min(step, nx - step))
     for step in order:
-        rs_out[step - 1] = part(step).astype(BF16)
+        rs_out[step - 1] = (parts[step] + part(step, 1 - core, normed[...])).astype(BF16)
         rs_copy(step).start()
-    total = part(0)
+    total = part(0, core, pass_out[core]) + part(0, 1 - core, normed[...])
     for step in reversed(order):
         rs_copy(step).wait_recv()
         total = total + rs_in[step - 1].astype(F32)
@@ -626,6 +675,7 @@
     for copy in swap:
         copy.wait_send()
     for h in heads:
+        decay_copy(h).wait_send()
         up_copy(h).wait_send()
 
     @pl.when(owns)
@@ -678,8 +728,10 @@
         pltpu.VMEM((2, rows, half), BF16),
         pltpu.VMEM((2, rows, half), BF16),
         pltpu.VMEM((2, rows, half_v), BF16),
-        pltpu.VMEM((nz // 2,) + message, BF16),
-        pltpu.VMEM((nz,) + message, BF16),
+        pltpu.VMEM((nz // 2, 8, 128), F32),
+        pltpu.VMEM((nz, 8, 128), F32),
+        pltpu.VMEM((nz // 2, DK, DK + DV), BF16),
+        pltpu.VMEM((nz, DK, DK + DV), BF16),
         pltpu.VMEM((ny,) + message, BF16),
         pltpu.VMEM((nz, DK, DV), F32),
         pltpu.VMEM((nz, DK, DK), BF16),
@@ -689,8 +741,9 @@
         pltpu.VMEM((nz // 2, DK, DV), BF16),
         pltpu.VMEM((nz // 2, 2 * rows, 2 * DK), BF16),
         pltpu.VMEM((nz // 2, 2 * rows, DV), F32),
+        pltpu.VMEM((rows, half_v), BF16),
         pltpu.VMEM((2, rows, half_v), BF16),
-        pltpu.VMEM((2, rows, half_v), BF16),
+        pltpu.VMEM((2, rows, half_v), F32),
         pltpu.VMEM((nx - 1, rows, width), BF16),
         pltpu.VMEM((nx - 1, rows, width), BF16),
         dma((13,)),
@@ -698,6 +751,8 @@
         dma((6,)),
         dma((6,)),
         dma((3,)),
+        dma((nz // 2,)),
+        dma((nz,)),
         dma((nz // 2,)),
         dma((nz,)),
         dma((ny,)),

time: 45.9 us -> 44.7 us (0.974)
  Pallas kernels: 45.1 us -> 43.9 us
    pallas_call x1, Pallas kernels: 45.1 us -> 43.9 us  [shards(): call(*(pltpu.with_memory_space_constraint(value, pltpu.HBM) for value in...]
where the time goes in v4:
time: 44.7 us; the launch traced here: 44.6 us
  Pallas kernels  43.9 us (98%)
  local copies, waits for them, and re-layouts  0.71 us (2%)
    pallas_call x1, Pallas kernels, shards(): call(*(pltpu.with_memory_space_constraint(value, pltpu.HBM) for value in...  43.9 us

profile of v4, /device:TPU:25, one launch (start us, length us, event | category | flops | bytes accessed | tf_op | source)
XLA Modules:
  0.0 44.6 jit_solution(5161442160857290564)
XLA Ops:
  0.0 43.9 %shard_map.127 = f32[128,512]{1,0:T(8,128)S(1)} custom-call(bf16[128,512]{1,0:T(8,128)(2,1)} %q_hbm.1, bf16[128,512]{1,0:T(8,128)(2,1)} %k_hbm.1, bf16[128,1024]{1,0:T(8,128)(2,1)} %v_hbm.1, bf16[128,1024]{1,0:T(8,128)(2,1)} %z_hbm.1, bf16[1024,2048]{1,0:T(8,128)(2,1)} %w_hbm.1, f32[8,128]{1,0:T(8,128)} %bitcast.5, f32[8,128]{1,0:T(8,128)} %bitcast.6, ...), custom_call_target="tpu_custom_call" | custom-call | flops 2000000000 | bytes 6000000 | tf_op jit(solution)/shard_map/pallas_call | solution.py:794
  43.9 0.7 %copy.15 = f32[128,512]{1,0:T(8,128)} copy(f32[128,512]{1,0:T(8,128)S(1)} %shard_map.127) | data formatting | bytes 524288

commit v5 on v4

--- a/solution.py
+++ b/solution.py
@@ -120,6 +120,8 @@
     normed,
     pass_out,
     gates,
+    relay_out,
+    relay_in,
     rs_out,
     rs_in,
     load_sem,
@@ -202,24 +204,24 @@
     def greet(ctx, heads):
         pl.semaphore_signal(barrier, inc=1, device_id=(ctx, heads), device_id_type=MESH)
 
-    for step in range(1, ring):
+    over = jnp.logical_and(place == ring - 1, me < count - 1)
+    under = jnp.logical_and(z == 0, y > 0)
+
+    @pl.when(over)
+    def _():
+        greet(me + 1, x)
+        greet(me + 2, x)
+
+    @pl.when(under)
+    def _():
+        greet(y * ring - 1, x)
+
+    for step in sorted(range(1, ring), key=lambda step: (min(step, ring - step), -step)):
         greet(y * ring + lax.rem(place + step, ring), x)
     for step in range(1, ny):
         greet(lax.rem(me + step * ring, count), x)
     for step in range(1, nx):
         greet(me, lax.rem(x + step, nx))
-    over = jnp.logical_and(place == ring - 1, me < count - 1)
-    under = jnp.logical_and(z == 0, y > 0)
-
-    @pl.when(over)
-    def _():
-        greet(me + 1, x)
-        greet(me + 2, x)
-
-    @pl.when(under)
-    def _():
-        greet(y * ring - 1, x)
-
     pl.semaphore_wait(
         barrier,
         (ring - 1) + (ny - 1) + (nx - 1) + 2 * over.astype(jnp.int32) + under.astype(jnp.int32),
@@ -636,7 +638,7 @@
         depth_rows = pl.ds(pl.multiple_of(which * depth, 128), depth)
         return mm(operand, w_in[depth_rows, cols_of(lax.rem(x + step, nx), width)])
 
-    order = sorted(range(1, nx), key=lambda step: -min(step, nx - step))
+    order = (2, 1, nx - 1)
     parts = {step: part(step, core, pass_out[core]) for step in order}
     pltpu.make_async_remote_copy(
         src_ref=pass_out.at[core],
@@ -647,24 +649,69 @@
         device_id_type=MESH,
     ).wait_recv()
 
-    def rs_copy(step):
+    def rs_copy(i, source, target, step):
         return pltpu.make_async_remote_copy(
-            src_ref=rs_out.at[step - 1],
-            dst_ref=rs_in.at[step - 1],
-            send_sem=rs_send.at[step - 1],
-            recv_sem=rs_recv.at[step - 1],
+            src_ref=source,
+            dst_ref=target,
+            send_sem=rs_send.at[i],
+            recv_sem=rs_recv.at[i],
             device_id=(me, lax.rem(x + step, nx)),
             device_id_type=MESH,
         )
 
-    for step in order:
-        rs_out[step - 1] = (parts[step] + part(step, 1 - core, normed[...])).astype(BF16)
-        rs_copy(step).start()
+    quarter = width // 4
+    ahead, back, across = 0, 1, 2
+    relays = [
+        rs_copy(i, relay_out.at[i], relay_in.at[i], step) for i, step in ((0, 1), (1, nx - 1))
+    ]
+    direct = rs_copy(2, rs_out.at[across, pl.ds(1, 2)], rs_in.at[across, pl.ds(1, 2)], 2)
+    early = [
+        rs_copy(3, rs_out.at[ahead, pl.ds(1, 3)], rs_in.at[ahead, pl.ds(1, 3)], 1),
+        rs_copy(4, rs_out.at[back, pl.ds(0, 3)], rs_in.at[back, pl.ds(0, 3)], nx - 1),
+    ]
+    late = [
+        rs_copy(5, rs_out.at[ahead, 0], rs_in.at[ahead, 0], 1),
+        rs_copy(6, rs_out.at[back, 3], rs_in.at[back, 3], nx - 1),
+    ]
+
+    def block(step):
+        whole = parts[step] + part(step, 1 - core, normed[...])
+        return [whole[:, i * quarter : (i + 1) * quarter] for i in range(4)]
+
+    pieces = block(2)
+    relay_out[0] = pieces[0].astype(BF16)
+    relays[0].start()
+    relay_out[1] = pieces[3].astype(BF16)
+    relays[1].start()
+    rs_out[across, 1] = pieces[1].astype(BF16)
+    rs_out[across, 2] = pieces[2].astype(BF16)
+    direct.start()
+    pieces = block(1)
+    for i in (1, 2, 3):
+        rs_out[ahead, i] = pieces[i].astype(BF16)
+    early[0].start()
+    waiting = [pieces[0]]
+    pieces = block(nx - 1)
+    for i in (0, 1, 2):
+        rs_out[back, i] = pieces[i].astype(BF16)
+    early[1].start()
+    waiting.append(pieces[3])
+    for i, (side, where) in enumerate(((ahead, 0), (back, 3))):
+        relays[i].wait_recv()
+        rs_out[side, where] = (waiting[i] + relay_in[i].astype(F32)).astype(BF16)
+        late[i].start()
     total = part(0, core, pass_out[core]) + part(0, 1 - core, normed[...])
-    for step in reversed(order):
-        rs_copy(step).wait_recv()
-        total = total + rs_in[step - 1].astype(F32)
-    out_ref[...] = total
+    for copy in early:
+        copy.wait_recv()
+    direct.wait_recv()
+    for copy in late:
+        copy.wait_recv()
+    for i in range(4):
+        cols = slice(i * quarter, (i + 1) * quarter)
+        piece = total[:, cols] + rs_in[ahead, i].astype(F32) + rs_in[back, i].astype(F32)
+        if i in (1, 2):
+            piece = piece + rs_in[across, i].astype(F32)
+        out_ref[:, cols] = piece
 
     @pl.when(sends_halo)
     def _():
@@ -689,8 +736,8 @@
                 carry_copy(y, later).wait_send()
 
     hand_over.wait_send()
-    for step in order:
-        rs_copy(step).wait_send()
+    for copy in relays + early + late + [direct]:
+        copy.wait_send()
 
 
 def shards(
@@ -744,8 +791,10 @@
         pltpu.VMEM((rows, half_v), BF16),
         pltpu.VMEM((2, rows, half_v), BF16),
         pltpu.VMEM((2, rows, half_v), F32),
-        pltpu.VMEM((nx - 1, rows, width), BF16),
-        pltpu.VMEM((nx - 1, rows, width), BF16),
+        pltpu.VMEM((2, rows, width // 4), BF16),
+        pltpu.VMEM((2, rows, width // 4), BF16),
+        pltpu.VMEM((3, 4, rows, width // 4), BF16),
+        pltpu.VMEM((3, 4, rows, width // 4), BF16),
         dma((13,)),
         dma((6,)),
         dma((6,)),
@@ -760,8 +809,8 @@
         dma((nz,)),
         dma((nz // 2,)),
         dma((2,)),
-        dma((nx - 1,)),
-        dma((nx - 1,)),
+        dma((7,)),
+        dma((7,)),
     ]
     call = pl.pallas_call(
         functools.partial(kernel, nx, ny, nz),

time: 44.7 us -> 43.8 us (0.980); the launches traced: 44.6 us -> 43.2 us
  Pallas kernels: 43.9 us -> 42.5 us
    pallas_call x1, Pallas kernels: 43.9 us -> 42.5 us  [shards(): call(*(pltpu.with_memory_space_constraint(value, pltpu.HBM) for value in...]
where the time goes in v5:
time: 43.8 us; the launch traced here: 43.2 us
  Pallas kernels  42.5 us (97%)
  local copies, waits for them, and re-layouts  0.71 us (2%)
    pallas_call x1, Pallas kernels, shards(): call(*(pltpu.with_memory_space_constraint(value, pltpu.HBM) for value in...  42.5 us

profile of v5, /device:TPU:25, one launch (start us, length us, event | category | flops | bytes accessed | tf_op | source)
XLA Modules:
  0.0 43.2 jit_solution(10931037993782292349)
XLA Ops:
  0.0 42.5 %shard_map.127 = f32[128,512]{1,0:T(8,128)S(1)} custom-call(bf16[128,512]{1,0:T(8,128)(2,1)} %q_hbm.1, bf16[128,512]{1,0:T(8,128)(2,1)} %k_hbm.1, bf16[128,1024]{1,0:T(8,128)(2,1)} %v_hbm.1, bf16[128,1024]{1,0:T(8,128)(2,1)} %z_hbm.1, bf16[1024,2048]{1,0:T(8,128)(2,1)} %w_hbm.1, f32[8,128]{1,0:T(8,128)} %bitcast.5, f32[8,128]{1,0:T(8,128)} %bitcast.6, ...), custom_call_target="tpu_custom_call" | custom-call | flops 2000000000 | bytes 6000000 | tf_op jit(solution)/shard_map/pallas_call | solution.py:843
  42.5 0.7 %copy.15 = f32[128,512]{1,0:T(8,128)} copy(f32[128,512]{1,0:T(8,128)S(1)} %shard_map.127) | data formatting | bytes 524288

commit v6 on v5

--- a/solution.py
+++ b/solution.py
@@ -108,7 +108,8 @@
     decay_in,
     up_out,
     up_in,
-    carry,
+    carry_state,
+    carry_map,
     pre_state,
     pre_map,
     pre_decay,
@@ -493,15 +494,27 @@
         reads[h, u * rows : (u + 1) * rows, 0:DK] = high
         reads[h, u * rows : (u + 1) * rows, DK:] = low
 
-    def carry_copy(source, target_y):
+    def carry_copy(source, target_y, i):
+        held = (carry_state, carry_map)[i]
         return pltpu.make_async_remote_copy(
-            src_ref=carry.at[source],
-            dst_ref=carry.at[source],
-            send_sem=y_send.at[target_y],
-            recv_sem=y_recv.at[source],
+            src_ref=held.at[source],
+            dst_ref=held.at[source],
+            send_sem=y_send.at[i * ny + target_y],
+            recv_sem=y_recv.at[i * ny + source],
             device_id=(target_y * ring + place, x),
             device_id_type=MESH,
         )
+
+    def each_carry(act):
+        for later in range(1, ny):
+
+            @pl.when(y < later)
+            def _(later=later):
+                act(carry_copy(y, later, 0))
+
+                @pl.when(y > 0)
+                def _():
+                    act(carry_copy(y, later, 1))
 
     def down_copy(target):
         slot = lax.rem(z, set_heads)
@@ -559,14 +572,10 @@
                 after((start, start + size), (start + size, start + 2 * size))
             size *= 2
         carried, total_decay = spans[0, nz]
-        put_maps(carry.at[y], carried, total_decay)
-        carry[y, DK:, :] = pack_decay(total_decay[:, 0:1], DK + DV)
-
-        for later in range(1, ny):
-
-            @pl.when(y < later)
-            def _(later=later):
-                carry_copy(y, later).start()
+        carry_state[y] = carried[:, 0:DV].astype(BF16)
+        carry_map[y, 0:DK, :] = map_of(carried, total_decay).astype(BF16)
+        carry_map[y, DK:, :] = pack_decay(total_decay[:, 0:1], DK)
+        each_carry(lambda copy: copy.start())
 
         for j in range(1, nz):
             if (0, j) not in spans:
@@ -582,14 +591,18 @@
 
             @pl.when(y > earlier)
             def _(earlier=earlier):
-                carry_copy(earlier, y).wait_recv()
-                message = carry[earlier]
-                state = sigma[...]
-                sigma[...] = (
-                    decay_of(message[DK:, 0:DV]) * state
-                    - mm(message[0:DK, DV:], state.astype(BF16))
-                    + message[0:DK, 0:DV].astype(F32)
-                )
+                carry_copy(earlier, y, 0).wait_recv()
+                fresh = carry_state[earlier].astype(F32)
+                if earlier == 0:
+                    sigma[...] = fresh
+                else:
+                    carry_copy(earlier, y, 1).wait_recv()
+                    state = sigma[...]
+                    sigma[...] = (
+                        decay_of(carry_map[earlier, DK:, :]) * state
+                        - mm(carry_map[earlier, 0:DK, :], state.astype(BF16))
+                        + fresh
+                    )
 
         start_state = sigma[...]
         rounded = start_state.astype(BF16)
@@ -729,11 +742,7 @@
     def _():
         for target in range(nz):
             down_copy(target).wait_send()
-        for later in range(1, ny):
-
-            @pl.when(y < later)
-            def _(later=later):
-                carry_copy(y, later).wait_send()
+        each_carry(lambda copy: copy.wait_send())
 
     hand_over.wait_send()
     for copy in relays + early + late + [direct]:
@@ -753,7 +762,6 @@
     hbm = pl.BlockSpec(memory_space=pltpu.HBM)
     vmem = pl.BlockSpec(memory_space=pltpu.VMEM)
     dma = pltpu.SemaphoreType.DMA
-    message = (DK + TAIL, DK + DV)
     scratch = [
         pltpu.VMEM((2, rows, half), BF16),
         pltpu.VMEM((2, rows, half), BF16),
@@ -779,7 +787,8 @@
         pltpu.VMEM((nz, 8, 128), F32),
         pltpu.VMEM((nz // 2, DK, DK + DV), BF16),
         pltpu.VMEM((nz, DK, DK + DV), BF16),
-        pltpu.VMEM((ny,) + message, BF16),
+        pltpu.VMEM((ny, DK, DV), BF16),
+        pltpu.VMEM((ny, DK + TAIL, DK), BF16),
         pltpu.VMEM((nz, DK, DV), F32),
         pltpu.VMEM((nz, DK, DK), BF16),
         pltpu.VMEM((nz, 8, 128), F32),
@@ -804,8 +813,8 @@
         dma((nz,)),
         dma((nz // 2,)),
         dma((nz,)),
-        dma((ny,)),
-        dma((ny,)),
+        dma((2 * ny,)),
+        dma((2 * ny,)),
         dma((nz,)),
         dma((nz // 2,)),
         dma((2,)),

time: 43.8 us -> 43.8 us (level)
  no operation moved by 1% of the time
where the time goes in v6:
time: 43.8 us; the launch traced here: 43.2 us
  Pallas kernels  42.5 us (97%)
  local copies, waits for them, and re-layouts  0.71 us (2%)
    pallas_call x1, Pallas kernels, shards(): call(*(pltpu.with_memory_space_constraint(value, pltpu.HBM) for value in...  42.5 us

profile of v6, /device:TPU:25, one launch (start us, length us, event | category | flops | bytes accessed | tf_op | source)
XLA Modules:
  0.0 43.2 jit_solution(16073009247477274722)
XLA Ops:
  0.0 42.5 %shard_map.127 = f32[128,512]{1,0:T(8,128)S(1)} custom-call(bf16[128,512]{1,0:T(8,128)(2,1)} %q_hbm.1, bf16[128,512]{1,0:T(8,128)(2,1)} %k_hbm.1, bf16[128,1024]{1,0:T(8,128)(2,1)} %v_hbm.1, bf16[128,1024]{1,0:T(8,128)(2,1)} %z_hbm.1, bf16[1024,2048]{1,0:T(8,128)(2,1)} %w_hbm.1, f32[8,128]{1,0:T(8,128)} %bitcast.5, f32[8,128]{1,0:T(8,128)} %bitcast.6, ...), custom_call_target="tpu_custom_call" | custom-call | flops 2000000000 | bytes 6000000 | tf_op jit(solution)/shard_map/pallas_call | solution.py:852
  42.5 0.7 %copy.15 = f32[128,512]{1,0:T(8,128)} copy(f32[128,512]{1,0:T(8,128)S(1)} %shard_map.127) | data formatting | bytes 524288

commit v7 on v6

--- a/solution.py
+++ b/solution.py
@@ -197,7 +197,7 @@
     ]
     first = [0, 1, 2, 8, 9, 10, 4, 5, 6, 7]
     rest = [3, 11, 12]
-    for i in first + rest:
+    for i in first:
         loads[i].start()
 
     barrier = pltpu.get_barrier_semaphore()
@@ -306,6 +306,8 @@
 
     for i in range(3):
         swapped[i].wait_recv()
+    for i in rest:
+        loads[i].start()
     for _, data, _, taps_ref, result, size in streams:
         result[1 - core] = conv(jnp.zeros((8, size), F32), data[1 - core], taps_ref, size)
 

time: 43.8 us -> 43.8 us (level)
  no operation moved by 1% of the time
where the time goes in v7:
time: 43.8 us; the launch traced here: 43.3 us
  Pallas kernels  42.5 us (97%)
  local copies, waits for them, and re-layouts  0.71 us (2%)
    pallas_call x1, Pallas kernels, shards(): call(*(pltpu.with_memory_space_constraint(value, pltpu.HBM) for value in...  42.5 us

profile of v7, /device:TPU:25, one launch (start us, length us, event | category | flops | bytes accessed | tf_op | source)
XLA Modules:
  0.0 43.3 jit_solution(5628173826246560602)
XLA Ops:
  0.0 42.5 %shard_map.127 = f32[128,512]{1,0:T(8,128)S(1)} custom-call(bf16[128,512]{1,0:T(8,128)(2,1)} %q_hbm.1, bf16[128,512]{1,0:T(8,128)(2,1)} %k_hbm.1, bf16[128,1024]{1,0:T(8,128)(2,1)} %v_hbm.1, bf16[128,1024]{1,0:T(8,128)(2,1)} %z_hbm.1, bf16[1024,2048]{1,0:T(8,128)(2,1)} %w_hbm.1, f32[8,128]{1,0:T(8,128)} %bitcast.5, f32[8,128]{1,0:T(8,128)} %bitcast.6, ...), custom_call_target="tpu_custom_call" | custom-call | flops 2000000000 | bytes 6000000 | tf_op jit(solution)/shard_map/pallas_call | solution.py:854
  42.5 0.7 %copy.15 = f32[128,512]{1,0:T(8,128)} copy(f32[128,512]{1,0:T(8,128)S(1)} %shard_map.127) | data formatting | bytes 524288
